TPU v7x, 128 devices: a whole 4x4x4 slice. The times are simulated.
128 devices in a mesh: section: 2 (over y_lo), row: 4 (over x), col: 16 (over y_hi, z, core).
Axes of the slice: x: 4, y: 4 (y_hi: 2, y_lo: 2; y = y_hi * 2 + y_lo), z: 4, core: 2. Of those that a mesh axis runs over, the one named last changes fastest.
Arguments:
- ends_in: bfloat16 [2, 2, 16, 256, 1024], P('section', None, 'col', 'row'), may hold values from -6 to 6
- q_weight: bfloat16 [2, 1024, 1024], P('section', 'col', 'row'), may hold values from -1.5 to 1.5
- key_projection: bfloat16 [2, 1024, 512], P('section', 'col', 'row'), may hold values from -0.1875 to 0.1875
- value_projection: bfloat16 [2, 1024, 512], P('section', 'col', 'row'), may hold values from -0.1875 to 0.1875
- out_weight: bfloat16 [2, 1024, 1024], P('section', 'col', 'row'), may hold values from -3 to 3
- attn_gain: float32 [2, 1024], P('section'), may hold values from 0.5 to 1.5
- moe_gain: float32 [2, 1024], P('section'), may hold values from 0.5 to 1.5
- gate_weight: bfloat16 [2, 32, 1024, 512], P('section', 'col'), may hold values from -0.1875 to 0.1875
- up_weight: bfloat16 [2, 32, 1024, 512], P('section', 'col'), may hold values from -0.1875 to 0.1875
- down_weight: bfloat16 [2, 32, 512, 1024], P('section', 'col'), may hold values from -3 to 3
- routes: int32 [2, 2, 16, 256, 8], P('section', None, 'col', 'row'), may hold values from 0 to 31, all different within a row; in each aligned block of 64 rows (0 to 63, 64 to 127, ..., all dimensions but the last counted through in order) at most 24 rows name the same one
- gates: float32 [2, 2, 16, 256, 8], P('section', None, 'col', 'row'), may hold values from 0.06 to 0.19
- lengths: int32 [2, 16, 4], P(None, 'col'), may hold values from 1 to 193, 256 in all within a row
Outputs:
- ends_out: bfloat16 [2, 2, 16, 256, 1024], P('section', None, 'col', 'row')
- grad_q_weight: float32 [2, 1024, 1024], P('section', 'col', 'row')
- grad_k_weight: float32 [2, 1024, 512], P('section', 'col', 'row')
- grad_v_weight: float32 [2, 1024, 512], P('section', 'col', 'row')
- grad_out_weight: float32 [2, 1024, 1024], P('section', 'col', 'row')
- grad_attn_gain: float32 [2, 1024], P('section')
- grad_moe_gain: float32 [2, 1024], P('section')
- grad_gate_weight: float32 [2, 32, 1024, 512], P('section', 'col', 'row')
- grad_up_weight: float32 [2, 32, 1024, 512], P('section', 'col', 'row')
- grad_down_weight: float32 [2, 32, 512, 1024], P('section', 'col', None, 'row')
Inputs may be any that keep to these rules, and one draw needn't show every extreme that they name: In each aligned block of 64 tokens (rows of all leading dimensions in order; the tokens of one device), no expert is named by more than 24 routes, one by exactly 24; a token's 8 routes are different experts. Each pack's 4 lengths sum to 256; the longest is exactly 193.
All inputs are finite; a program needn't handle non-finite values.
Results may differ from a plain program's by a relative error of at most 0.03.
Values may be sent and summed in bfloat16 or wider, within the bound.
A program may use at most 128 MiB of HBM per device.

v0:
```python
import jax
import jax.numpy as jnp
from jax import lax
from jax.sharding import PartitionSpec as P

HEAD_SIZE = 64


SCORE_MUL = 0.015625
RESID_MUL = 0.22
NORM_EPS = 1e-06
ROPE_THETA = 10000.0


def shifted(value, axis, steps):
    count = lax.axis_size(axis)
    leading, last = (max(0, -steps), min(count, count - steps))
    return lax.ppermute(value, axis, [(source, source + steps) for source in range(leading, last)])


def layout_tables(length_row, row_count, head_width):
    ends_at = jnp.cumsum(length_row)
    places = jnp.arange(row_count, dtype=jnp.int32)
    passed = places[:, None] >= ends_at[None, :]
    segment = jnp.sum(passed.astype(jnp.int32), axis=1)
    starts = jnp.sum(jnp.where(passed, length_row[None, :], 0), axis=1)
    offset = (places - starts).astype(jnp.float32)
    frequency = ROPE_THETA ** (-(jnp.arange(head_width // 2, dtype=jnp.float32) * 2.0 / head_width))
    angles = offset[:, None] * frequency[None, :]
    cosine_table = jnp.concatenate([jnp.cos(angles), jnp.cos(angles)], axis=1)[:, None, :]
    sine_table = jnp.concatenate([jnp.sin(angles), jnp.sin(angles)], axis=1)[:, None, :]
    allowed = (segment[:, None] == segment[None, :]) & (places[None, :] <= places[:, None])
    return (cosine_table, sine_table, allowed)


def turn_half(values):
    middle = values.shape[-1] // 2
    return jnp.concatenate([-values[..., middle:], values[..., :middle]], axis=-1)


def turn_back(values):
    middle = values.shape[-1] // 2
    return jnp.concatenate([values[..., middle:], -values[..., :middle]], axis=-1)


def rotary(values, cosine_table, sine_table):
    return values * cosine_table + turn_half(values) * sine_table


def rotary_back(gradient, cosine_table, sine_table):
    return gradient * cosine_table + turn_back(gradient * sine_table)


def attend(query_token_rows, key_rows, value_rows, allowed):
    row_count, head_count, head_width = query_token_rows.shape
    key_heads = key_rows.shape[1]
    grouped_heads = query_token_rows.reshape(
        row_count, key_heads, head_count // key_heads, head_width
    )
    scores = (
        jnp.einsum("qhgd,shd->hgqs", grouped_heads, key_rows, preferred_element_type=jnp.float32)
        * SCORE_MUL
    )
    scores = jnp.where(allowed, scores, -1e30)
    highest = jnp.max(scores, axis=-1, keepdims=True)
    weights = jnp.exp(scores - highest)
    totals = jnp.sum(weights, axis=-1, keepdims=True)
    log_total = highest + jnp.log(totals)
    probability = (weights / totals).astype(jnp.bfloat16)
    mixed = jnp.einsum(
        "hgqs,shd->qhgd", probability, value_rows, preferred_element_type=jnp.float32
    )
    return (mixed.reshape(row_count, head_count * head_width).astype(jnp.bfloat16), log_total)


def attend_back(query_token_rows, key_rows, value_rows, allowed, log_total, grad_mixed):
    row_count, head_count, head_width = query_token_rows.shape
    key_heads = key_rows.shape[1]
    grouped_heads = query_token_rows.reshape(
        row_count, key_heads, head_count // key_heads, head_width
    )
    grad_grouped = grad_mixed.reshape(row_count, key_heads, head_count // key_heads, head_width)
    scores = (
        jnp.einsum("qhgd,shd->hgqs", grouped_heads, key_rows, preferred_element_type=jnp.float32)
        * SCORE_MUL
    )
    probability = jnp.where(allowed, jnp.exp(scores - log_total), 0.0)
    grad_value = jnp.einsum(
        "hgqs,qhgd->shd",
        probability.astype(jnp.bfloat16),
        grad_grouped,
        preferred_element_type=jnp.float32,
    )
    grad_prob = jnp.einsum(
        "qhgd,shd->hgqs", grad_grouped, value_rows, preferred_element_type=jnp.float32
    )
    grad_scores = probability * (
        grad_prob - jnp.sum(probability * grad_prob, axis=-1, keepdims=True)
    )
    grad_scores = grad_scores.astype(jnp.bfloat16)
    grad_query = (
        jnp.einsum("hgqs,shd->qhgd", grad_scores, key_rows, preferred_element_type=jnp.float32)
        * SCORE_MUL
    )
    grad_key = (
        jnp.einsum("hgqs,qhgd->shd", grad_scores, grouped_heads, preferred_element_type=jnp.float32)
        * SCORE_MUL
    )
    return (grad_query.reshape(row_count, head_count, head_width), grad_key, grad_value)


def routing(route_rows, expert_count, capacity):
    token_count, route_count = route_rows.shape
    flat_routes = route_rows.reshape(-1)
    chosen = (flat_routes[:, None] == jnp.arange(expert_count, dtype=jnp.int32)[None, :]).astype(
        jnp.int32
    )
    earlier = jnp.cumsum(chosen, axis=0) - chosen
    slot_index = jnp.sum(earlier * chosen, axis=1)
    target = flat_routes * capacity + slot_index
    placing = (
        target[:, None] == jnp.arange(expert_count * capacity, dtype=jnp.int32)[None, :]
    ).astype(jnp.bfloat16)
    dispatch = jnp.sum(placing.reshape(token_count, route_count, expert_count * capacity), axis=1)
    return (dispatch, placing)


def contract_rows(left_mat, right_mat):
    return lax.dot_general(
        left_mat, right_mat, (((0,), (0,)), ((), ())), preferred_element_type=jnp.float32
    )


def contract_cols(left_mat, right_mat):
    return lax.dot_general(
        left_mat, right_mat, (((1,), (1,)), ((), ())), preferred_element_type=jnp.float32
    )


def layer_forward(
    quarter_rows, attn_mats, gain_pair, expert_mats, route_rows, gate_rows, length_row
):
    query_full, key_full, value_full, output_full = attn_mats
    attn_gain_row, moe_gain_row = gain_pair
    gate_mats, up_mats, down_mats = expert_mats
    token_count, model_width = quarter_rows.shape
    head_width = HEAD_SIZE
    packed = lax.all_gather(quarter_rows, "row", axis=0, tiled=True)
    row_count = packed.shape[0]
    cosine_table, sine_table, allowed = layout_tables(length_row, row_count, head_width)
    packed_float = packed.astype(jnp.float32)
    scale_one = lax.rsqrt(jnp.mean(packed_float * packed_float, axis=1) + NORM_EPS)
    normed_one = (packed_float * scale_one[:, None] * attn_gain_row).astype(jnp.bfloat16)
    query_pre = jnp.dot(normed_one, query_full, preferred_element_type=jnp.float32).reshape(
        row_count, -1, head_width
    )
    key_before_rotary = jnp.dot(normed_one, key_full, preferred_element_type=jnp.float32).reshape(
        row_count, -1, head_width
    )
    value_before_heads = jnp.dot(
        normed_one, value_full, preferred_element_type=jnp.float32
    ).reshape(row_count, -1, head_width)
    query_token_rows = rotary(query_pre, cosine_table, sine_table).astype(jnp.bfloat16)
    key_rows = rotary(key_before_rotary, cosine_table, sine_table).astype(jnp.bfloat16)
    value_rows = value_before_heads.astype(jnp.bfloat16)
    mixed, log_total = attend(query_token_rows, key_rows, value_rows, allowed)
    partial_value = contract_cols(mixed, output_full)
    attended = lax.psum_scatter(
        partial_value.astype(jnp.bfloat16), "row", scatter_dimension=0, tiled=True
    ).astype(jnp.float32)
    resid = quarter_rows.astype(jnp.float32) + RESID_MUL * attended
    scale_two = lax.rsqrt(jnp.mean(resid * resid, axis=1) + NORM_EPS)
    normed_two = (resid * scale_two[:, None] * moe_gain_row).astype(jnp.bfloat16)
    expert_count = gate_mats.shape[0] * lax.axis_size("col")
    route_count = route_rows.shape[1]
    capacity = min(token_count, 3 * token_count * route_count // (2 * expert_count))
    dispatch, placing = routing(route_rows, expert_count, capacity)
    sending = contract_rows(dispatch, normed_two).astype(jnp.bfloat16)
    sending = sending.reshape(expert_count, capacity, model_width)
    arrived = lax.all_to_all(sending, "col", split_axis=0, concat_axis=1, tiled=True)
    gate_pre = jnp.einsum("erd,edf->erf", arrived, gate_mats, preferred_element_type=jnp.float32)
    up_pre = jnp.einsum("erd,edf->erf", arrived, up_mats, preferred_element_type=jnp.float32)
    hidden = (jax.nn.silu(gate_pre) * up_pre).astype(jnp.bfloat16)
    produced = jnp.einsum(
        "erf,efd->erd", hidden, down_mats, preferred_element_type=jnp.float32
    ).astype(jnp.bfloat16)
    returned = lax.all_to_all(produced, "col", split_axis=1, concat_axis=0, tiled=True)
    picked = jnp.dot(placing, returned.reshape(-1, model_width), preferred_element_type=jnp.float32)
    mixture = jnp.sum(
        picked.reshape(token_count, route_count, model_width) * gate_rows[:, :, None], axis=1
    )
    output_rows = (resid + RESID_MUL * mixture).astype(jnp.bfloat16)
    retained = (
        packed_float,
        scale_one,
        normed_one,
        query_token_rows,
        key_rows,
        value_rows,
        log_total,
        mixed,
        resid,
        scale_two,
        dispatch,
        placing,
        gate_rows,
        arrived,
        gate_pre,
        up_pre,
        hidden,
        allowed,
        cosine_table,
        sine_table,
    )
    return (output_rows, retained)


def layer_backward(retained, arriving_grad, attn_mats, gain_pair, expert_mats):
    (
        packed_float,
        scale_one,
        normed_one,
        query_token_rows,
        key_rows,
        value_rows,
        log_total,
        mixed,
        resid,
        scale_two,
        dispatch,
        placing,
        gate_rows,
        arrived,
        gate_pre,
        up_pre,
        hidden,
        allowed,
        cosine_table,
        sine_table,
    ) = retained
    query_full, key_full, value_full, output_full = attn_mats
    attn_gain_row, moe_gain_row = gain_pair
    gate_mats, up_mats, down_mats = expert_mats
    token_count, model_width = resid.shape
    row_count = packed_float.shape[0]
    expert_count = gate_mats.shape[0] * lax.axis_size("col")
    flowing = arriving_grad.astype(jnp.float32)
    route_grad = (
        (RESID_MUL * gate_rows[:, :, None] * flowing[:, None, :])
        .astype(jnp.bfloat16)
        .reshape(-1, model_width)
    )
    grad_back = (
        contract_rows(placing, route_grad)
        .astype(jnp.bfloat16)
        .reshape(expert_count, -1, model_width)
    )
    grad_produced = lax.all_to_all(grad_back, "col", split_axis=0, concat_axis=1, tiled=True)
    grad_down = jnp.einsum(
        "erf,erd->efd", hidden, grad_produced, preferred_element_type=jnp.float32
    )
    grad_hidden = jnp.einsum(
        "erd,efd->erf", grad_produced, down_mats, preferred_element_type=jnp.float32
    )
    sigmoid_gate = jax.nn.sigmoid(gate_pre)
    grad_gate = (
        grad_hidden * up_pre * sigmoid_gate * (1.0 + gate_pre * (1.0 - sigmoid_gate))
    ).astype(jnp.bfloat16)
    grad_up = (grad_hidden * gate_pre * sigmoid_gate).astype(jnp.bfloat16)
    grad_gate_mats = jnp.einsum(
        "erd,erf->edf", arrived, grad_gate, preferred_element_type=jnp.float32
    )
    grad_up_mats = jnp.einsum("erd,erf->edf", arrived, grad_up, preferred_element_type=jnp.float32)
    grad_arrived = jnp.einsum(
        "erf,edf->erd", grad_gate, gate_mats, preferred_element_type=jnp.float32
    )
    grad_arrived = grad_arrived + jnp.einsum(
        "erf,edf->erd", grad_up, up_mats, preferred_element_type=jnp.float32
    )
    grad_sent = lax.all_to_all(
        grad_arrived.astype(jnp.bfloat16), "col", split_axis=1, concat_axis=0, tiled=True
    )
    grad_normed_two = jnp.dot(
        dispatch, grad_sent.reshape(-1, model_width), preferred_element_type=jnp.float32
    )
    grad_moe_gain = jnp.sum(grad_normed_two * resid * scale_two[:, None], axis=0)
    weighted_two = grad_normed_two * moe_gain_row
    grad_resid = (
        flowing
        + scale_two[:, None] * weighted_two
        - resid * (scale_two**3)[:, None] * jnp.mean(weighted_two * resid, axis=1, keepdims=True)
    )
    grad_attended = (RESID_MUL * grad_resid).astype(jnp.bfloat16)
    grad_partial = lax.all_gather(grad_attended, "row", axis=0, tiled=True)
    grad_output_mat = contract_rows(grad_partial, mixed)
    grad_mixed = jnp.dot(grad_partial, output_full, preferred_element_type=jnp.float32).astype(
        jnp.bfloat16
    )
    grad_query, grad_key, grad_value = attend_back(
        query_token_rows,
        key_rows,
        value_rows,
        allowed,
        log_total,
        grad_mixed.reshape(query_token_rows.shape),
    )
    grad_query_pre = (
        rotary_back(grad_query, cosine_table, sine_table)
        .reshape(row_count, -1)
        .astype(jnp.bfloat16)
    )
    grad_key_pre = (
        rotary_back(grad_key, cosine_table, sine_table).reshape(row_count, -1).astype(jnp.bfloat16)
    )
    grad_value_pre = grad_value.reshape(row_count, -1).astype(jnp.bfloat16)
    grad_query_mat = contract_rows(normed_one, grad_query_pre)
    grad_key_mat = contract_rows(normed_one, grad_key_pre)
    grad_value_mat = contract_rows(normed_one, grad_value_pre)
    grad_normed_one = (
        contract_cols(grad_query_pre, query_full)
        + contract_cols(grad_key_pre, key_full)
        + contract_cols(grad_value_pre, value_full)
    )
    grad_attn_gain = jnp.sum(grad_normed_one * packed_float * scale_one[:, None], axis=0)
    weighted_one = grad_normed_one * attn_gain_row
    grad_packed = scale_one[:, None] * weighted_one - packed_float * (scale_one**3)[
        :, None
    ] * jnp.mean(weighted_one * packed_float, axis=1, keepdims=True)
    grad_quarter = (
        lax.psum_scatter(
            grad_packed.astype(jnp.bfloat16), "row", scatter_dimension=0, tiled=True
        ).astype(jnp.float32)
        + grad_resid
    )
    attn_grads = (grad_query_mat, grad_key_mat, grad_value_mat, grad_output_mat)
    gain_grads = (grad_attn_gain, grad_moe_gain)
    expert_grads = (grad_gate_mats, grad_up_mats, grad_down)
    return (grad_quarter, attn_grads, gain_grads, expert_grads)


def sum_attention(grads_four):
    return (
        lax.psum_scatter(
            grads_four[0].astype(jnp.bfloat16), "col", scatter_dimension=0, tiled=True
        ).astype(jnp.float32),
        lax.psum_scatter(
            grads_four[1].astype(jnp.bfloat16), "col", scatter_dimension=0, tiled=True
        ).astype(jnp.float32),
        lax.psum_scatter(
            grads_four[2].astype(jnp.bfloat16), "col", scatter_dimension=0, tiled=True
        ).astype(jnp.float32),
        lax.psum_scatter(
            grads_four[3].astype(jnp.bfloat16), "col", scatter_dimension=0, tiled=True
        ).astype(jnp.float32),
    )


def sum_experts(grads_three):
    return (
        lax.psum_scatter(
            grads_three[0].astype(jnp.bfloat16), "row", scatter_dimension=1, tiled=True
        ).astype(jnp.float32),
        lax.psum_scatter(
            grads_three[1].astype(jnp.bfloat16), "row", scatter_dimension=1, tiled=True
        ).astype(jnp.float32),
        lax.psum_scatter(
            grads_three[2].astype(jnp.bfloat16), "row", scatter_dimension=2, tiled=True
        ).astype(jnp.float32),
    )


def sum_gains(grads_two):
    return lax.psum((grads_two[0], grads_two[1]), ("row", "col"))


def add_trees(former, latter):
    return jax.tree.map(lambda left_part, right_part: left_part + right_part, former, latter)


def per_device(
    ends_in,
    q_weight,
    key_projection,
    value_projection,
    out_weight,
    attn_gain,
    moe_gain,
    gate_weight,
    up_weight,
    down_weight,
    routes,
    gates,
    lengths,
):
    attn_mats = (
        lax.all_gather(q_weight[0], "col", axis=0, tiled=True),
        lax.all_gather(key_projection[0], "col", axis=0, tiled=True),
        lax.all_gather(value_projection[0], "col", axis=0, tiled=True),
        lax.all_gather(out_weight[0], "col", axis=0, tiled=True),
    )
    gain_pair = (attn_gain[0], moe_gain[0])
    expert_mats = (gate_weight[0], up_weight[0], down_weight[0])
    section_index = lax.axis_index("section")
    on_first = section_index == 0
    local_ends = ends_in[0, :, 0]
    route_all = routes[0, :, 0]
    gate_all = gates[0, :, 0]
    length_all = lengths[:, 0]
    micro_count = local_ends.shape[0]
    arriving = jnp.zeros_like(local_ends[0])
    retained_list = []
    forward_rows = []
    for step_index in range(micro_count + 1):
        which_batch = jnp.clip(step_index - section_index, 0, micro_count - 1)
        entry_rows = jnp.where(on_first, local_ends[min(step_index, micro_count - 1)], arriving)
        output_rows, retained = layer_forward(
            entry_rows,
            attn_mats,
            gain_pair,
            expert_mats,
            route_all[which_batch],
            gate_all[which_batch],
            length_all[which_batch],
        )
        retained_list.append(retained)
        forward_rows.append(output_rows)
        if step_index < micro_count:
            arriving = shifted(output_rows, "section", 1)
    returning = jnp.zeros_like(local_ends[0])
    backward_rows = []
    totals = None
    for step_index in range(micro_count + 1):
        which_batch = step_index - 1 + section_index
        valid_flag = jnp.where((which_batch >= 0) & (which_batch < micro_count), 1.0, 0.0).astype(
            jnp.float32
        )
        early_kept = retained_list[max(step_index - 1, 0)]
        late_kept = retained_list[min(step_index + 1, micro_count)]
        chosen_kept = jax.tree.map(
            lambda former, latter: jnp.where(on_first, former, latter), early_kept, late_kept
        )
        entry_grad = jnp.where(on_first, returning, local_ends[min(step_index, micro_count - 1)])
        grad_quarter, attn_grads, gain_grads, expert_grads = layer_backward(
            chosen_kept, entry_grad, attn_mats, gain_pair, expert_mats
        )
        grad_rounded = grad_quarter.astype(jnp.bfloat16)
        backward_rows.append(grad_rounded)
        if step_index < micro_count:
            returning = shifted(grad_rounded, "section", -1)
        masked = jax.tree.map(
            lambda part_value: part_value * valid_flag, (attn_grads, gain_grads, expert_grads)
        )
        totals = masked if totals is None else add_trees(totals, masked)
    reduced = (sum_attention(totals[0]), sum_gains(totals[1]), sum_experts(totals[2]))
    ends_rows = [
        jnp.where(on_first, backward_rows[batch_index + 1], forward_rows[batch_index + 1])
        for batch_index in range(micro_count)
    ]
    ends_out = jnp.stack(ends_rows, axis=0)[None, :, None]
    attn_sums, gain_sums, expert_sums = reduced
    return (
        ends_out,
        attn_sums[0][None],
        attn_sums[1][None],
        attn_sums[2][None],
        attn_sums[3][None],
        gain_sums[0][None],
        gain_sums[1][None],
        expert_sums[0][None],
        expert_sums[1][None],
        expert_sums[2][None],
    )


def solution(mesh):
    placed = (
        P("section", None, "col", "row", None),
        P("section", "col", "row"),
        P("section", "col", "row"),
        P("section", "col", "row"),
        P("section", "col", "row"),
        P("section", None),
        P("section", None),
        P("section", "col", None, None),
        P("section", "col", None, None),
        P("section", "col", None, None),
        P("section", None, "col", "row", None),
        P("section", None, "col", "row", None),
        P(None, "col", None),
    )
    return jax.shard_map(
        per_device,
        mesh=mesh,
        in_specs=placed,
        out_specs=(
            P("section", None, "col", "row", None),
            P("section", "col", "row"),
            P("section", "col", "row"),
            P("section", "col", "row"),
            P("section", "col", "row"),
            P("section", None),
            P("section", None),
            P("section", "col", "row", None),
            P("section", "col", "row", None),
            P("section", "col", None, "row"),
        ),
        check_vma=False,
    )
```

profile of v0, /device:TPU:1, one launch (start us, length us, event | category | flops | bytes accessed | tf_op | source)
XLA Modules:
  0.0 1110.9 jit_solution(5404439545782050361)
XLA Ops:
  12.0 12.3 %all-gather = bf16[1,1,1,256,1024]{4,3,2,1,0:T(8,128)(2,1)S(1)} all-gather(bf16[1,1,1,64,1024]{4,3,2,1,0:T(8,128)(2,1)S(1)} %get-tuple-element.137), channel_id=2, replica_groups=mesh['section'=2,'row'=4,'col'=16] {'row'}, dimensions={3}, use_global_device_ids=true | all-gather | bytes 655360 | tf_op jit(solution)/shard_map/all_gather | solution.py:148
  24.6 28.4 %all-gather.2 = bf16[1,1024,128]{2,1,0:T(8,128)(2,1)S(1)} all-gather(bf16[1,64,128]{2,1,0:T(8,128)(2,1)S(1)} %copy-done.208), channel_id=4, replica_groups=mesh['section'=2,'row'=4,'col'=16] {'col'}, dimensions={1}, use_global_device_ids=true | all-gather | bytes 278528 | tf_op jit(solution)/shard_map/all_gather | solution.py:397
  53.8 20.7 %all-gather.3 = bf16[1,1024,256]{2,1,0:T(8,128)(2,1)S(1)} all-gather(bf16[1,64,256]{2,1,0:T(8,128)(2,1)S(1)} %copy-done.187), channel_id=5, replica_groups=mesh['section'=2,'row'=4,'col'=16] {'col'}, dimensions={1}, use_global_device_ids=true | all-gather | bytes 557056 | tf_op jit(solution)/shard_map/all_gather | solution.py:396
  75.0 21.3 %all-gather.1 = bf16[1,1024,128]{2,1,0:T(8,128)(2,1)S(1)} all-gather(bf16[1,64,128]{2,1,0:T(8,128)(2,1)S(1)} %copy-done.209), channel_id=3, replica_groups=mesh['section'=2,'row'=4,'col'=16] {'col'}, dimensions={1}, use_global_device_ids=true | all-gather | bytes 278528 | tf_op jit(solution)/shard_map/all_gather | solution.py:398
  96.8 20.7 %all-gather.4 = bf16[1,1024,256]{2,1,0:T(8,128)(2,1)S(1)} all-gather(bf16[1,64,256]{2,1,0:T(8,128)(2,1)S(1)} %copy-done.188), channel_id=6, replica_groups=mesh['section'=2,'row'=4,'col'=16] {'col'}, dimensions={1}, use_global_device_ids=true | all-gather | bytes 557056 | tf_op jit(solution)/shard_map/all_gather | solution.py:399
  127.2 13.6 %reduce-scatter.14.cloned.1.call-done = bf16[64,1024]{1,0:T(8,128)(2,1)} async-done(((bf16[256,1024]{1,0:T(8,128)(2,1)}), bf16[64,1024]{1,0:T(8,128)(2,1)}) %reduce-scatter.14.cloned.1.call-update) | async-done | bytes 131088 | tf_op jit(solution)/shard_map/reduce_scatter | solution.py:168
  143.5 31.6 %all_to_all.198 = bf16[32,24,1024]{2,1,0:T(8,128)(2,1)S(1)} all-to-all(bf16[32,24,1024]{2,1,0:T(8,128)(2,1)S(1)} %bitcast.726), channel_id=1, replica_groups=mesh['section'=2,'row'=4,'col'=16] {'col'}, dimensions={0} | all-to-all | bytes 3145728 | tf_op jit(solution)/shard_map/all_to_all | solution.py:180
  185.6 5.4 all-to-all-start.1
  195.8 18.3 %all-to-all-done.1 = bf16[2,384,1024]{2,0,1:T(2,128)(2,1)} async-done(((bf16[2,384,1024]{2,0,1:T(2,128)(2,1)}), bf16[2,384,1024]{2,0,1:T(2,128)(2,1)}, u32[]{:S(2)}, u32[]{:S(2)}) %all-to-all-start.1) | async-done | bytes 1572896 | tf_op jit(solution)/shard_map/all_to_all | solution.py:187
  221.9 10.3 all_gather.35
  238.0 3.4 convolution_convert_fusion.3
  241.4 9.7 all-to-all-start.4
  254.9 7.0 reduce-scatter.16.cloned.1.call-done
  267.4 6.6 all-to-all-done.4
  274.0 5.8 all-to-all-start.2
  282.5 20.1 %all-to-all-done.2 = bf16[32,24,1024]{2,1,0:T(8,128)(2,1)} async-done(((bf16[32,24,1024]{2,1,0:T(8,128)(2,1)}), bf16[32,24,1024]{2,1,0:T(8,128)(2,1)}, u32[]{:S(2)}, u32[]{:S(2)}) %all-to-all-start.2) | async-done | bytes 1572896 | tf_op jit(solution)/shard_map/all_to_all | solution.py:180
  309.9 2.8 multiply_convert_fusion.6
  315.0 2.8 copy.224
  317.8 5.3 all-to-all-start.5
  328.0 18.1 %all-to-all-done.5 = bf16[2,384,1024]{2,0,1:T(2,128)(2,1)} async-done(((bf16[2,384,1024]{2,0,1:T(2,128)(2,1)}), bf16[2,384,1024]{2,0,1:T(2,128)(2,1)}, u32[]{:S(2)}, u32[]{:S(2)}) %all-to-all-start.5) | async-done | bytes 1572896 | tf_op jit(solution)/shard_map/all_to_all | solution.py:280
  346.1 5.3 all-to-all-start.3
  357.4 16.9 %all-to-all-done.3 = bf16[2,384,1024]{2,0,1:T(2,128)(2,1)} async-done(((bf16[2,384,1024]{2,0,1:T(2,128)(2,1)}), bf16[2,384,1024]{2,0,1:T(2,128)(2,1)}, u32[]{:S(2)}, u32[]{:S(2)}) %all-to-all-start.3) | async-done | bytes 1572896 | tf_op jit(solution)/shard_map/all_to_all | solution.py:187
  380.3 10.0 all_gather.37
  401.6 3.8 collective-permute-start.1
  405.4 14.0 %reduce-scatter.18.cloned.1.call-done = bf16[64,1024]{1,0:T(8,128)(2,1)} async-done(((bf16[256,1024]{1,0:T(8,128)(2,1)}), bf16[64,1024]{1,0:T(8,128)(2,1)}) %reduce-scatter.18.cloned.1.call-update) | async-done | bytes 131088 | tf_op jit(solution)/shard_map/reduce_scatter | solution.py:330
  423.2 3.1 collective-permute-done.2
  427.1 10.4 all_gather.36
  445.0 3.4 convolution_convert_fusion.2
  448.4 13.3 %all-to-all-start.6 = ((bf16[32,24,1024]{2,1,0:T(8,128)(2,1)}), bf16[32,24,1024]{2,1,0:T(8,128)(2,1)}, u32[]{:S(2)}, u32[]{:S(2)}) async-start(bf16[32,24,1024]{2,1,0:T(8,128)(2,1)} %bitcast.739), calls=%async_computation.10 | async-start | bytes 3145728 | tf_op jit(solution)/shard_map/all_to_all | solution.py:258
  465.6 4.5 reduce-scatter.20.cloned.1.call-done
  475.1 9.4 all-to-all-done.6
  484.5 5.3 all-to-all-start.7
  492.5 20.2 %all-to-all-done.7 = bf16[32,24,1024]{2,1,0:T(8,128)(2,1)} async-done(((bf16[32,24,1024]{2,1,0:T(8,128)(2,1)}), bf16[32,24,1024]{2,1,0:T(8,128)(2,1)}, u32[]{:S(2)}, u32[]{:S(2)}) %all-to-all-start.7) | async-done | bytes 1572896 | tf_op jit(solution)/shard_map/all_to_all | solution.py:180
  523.9 2.8 copy.236
  526.7 5.2 all-to-all-start.8
  533.3 21.6 %all-to-all-done.8 = bf16[2,384,1024]{2,0,1:T(2,128)(2,1)} async-done(((bf16[2,384,1024]{2,0,1:T(2,128)(2,1)}), bf16[2,384,1024]{2,0,1:T(2,128)(2,1)}, u32[]{:S(2)}, u32[]{:S(2)}) %all-to-all-start.8) | async-done | bytes 1572896 | tf_op jit(solution)/shard_map/all_to_all | solution.py:280
  559.3 10.0 all_gather.38
  575.6 20.9 %reduce-scatter.22.cloned.1.call-done = bf16[64,1024]{1,0:T(8,128)(2,1)} async-done(((bf16[256,1024]{1,0:T(8,128)(2,1)}), bf16[64,1024]{1,0:T(8,128)(2,1)}) %reduce-scatter.22.cloned.1.call-update) | async-done | bytes 131088 | tf_op jit(solution)/shard_map/reduce_scatter | solution.py:330
  605.2 3.1 convolution_convert_fusion
  608.3 10.7 all-to-all-start.9
  619.0 5.0 fusion.135
  628.7 13.1 %all-to-all-done.9 = bf16[32,24,1024]{2,1,0:T(8,128)(2,1)} async-done(((bf16[32,24,1024]{2,1,0:T(8,128)(2,1)}), bf16[32,24,1024]{2,1,0:T(8,128)(2,1)}, u32[]{:S(2)}, u32[]{:S(2)}) %all-to-all-start.9) | async-done | bytes 1572896 | tf_op jit(solution)/shard_map/all_to_all | solution.py:258
  644.1 4.8 multiply_convert_fusion.2
  652.1 2.8 copy.244
  654.9 5.3 all-to-all-start.10
  668.9 14.3 %all-to-all-done.10 = bf16[2,384,1024]{2,0,1:T(2,128)(2,1)} async-done(((bf16[2,384,1024]{2,0,1:T(2,128)(2,1)}), bf16[2,384,1024]{2,0,1:T(2,128)(2,1)}, u32[]{:S(2)}, u32[]{:S(2)}) %all-to-all-start.10) | async-done | bytes 1572896 | tf_op jit(solution)/shard_map/all_to_all | solution.py:280
  688.0 10.2 all_gather.39
  722.2 3.1 fusion.133
  726.0 2.9 add_convert_fusion
  730.1 2.9 fusion.152
  734.6 2.9 add_convert_fusion.1
  738.7 2.9 fusion.153
  743.2 3.0 add_convert_fusion.2
  748.3 2.8 copy.250
  751.1 8.9 all-to-all-start.11
  760.2 22.9 %all-to-all-done.11 = bf16[2,384,1024]{2,0,1:T(2,128)(2,1)} async-done(((bf16[2,384,1024]{2,0,1:T(2,128)(2,1)}), bf16[2,384,1024]{2,0,1:T(2,128)(2,1)}, u32[]{:S(2)}, u32[]{:S(2)}) %all-to-all-start.11) | async-done | bytes 1572896 | tf_op jit(solution)/shard_map/all_to_all | solution.py:187
  783.0 3.1 copy.251
  786.2 165.4 %all-reduce = (f32[1,1024]{1,0:T(1,128)}, f32[1,1024]{1,0:T(1,128)}) all-reduce(f32[1,1024]{1,0:T(1,128)S(1)} %bitcast.827, f32[1,1024]{1,0:T(1,128)S(1)} %bitcast.826), channel_id=1, replica_groups=mesh['section'=2,'row'=4,'col'=16] {'row','col'}, use_global_device_ids=true, to_apply=%region_58.59 | all-reduce | flops 2048 | bytes 16384 | tf_op jit(solution)/shard_map/psum | solution.py:373
  951.5 2.8 multiply_reduce_fusion
  958.5 22.8 %reduce-scatter.26.cloned.1.call-done = bf16[64,256]{1,0:T(8,128)(2,1)} async-done(((bf16[1024,256]{1,0:T(8,128)(2,1)}), bf16[64,256]{1,0:T(8,128)(2,1)}) %reduce-scatter.26.cloned.1.call-update) | async-done | bytes 32784 | tf_op jit(solution)/shard_map/reduce_scatter | solution.py:343
  982.6 21.9 %reduce-scatter.24.cloned.1.call-done = bf16[64,1024]{1,0:T(8,128)(2,1)} async-done(((bf16[256,1024]{1,0:T(8,128)(2,1)}), bf16[64,1024]{1,0:T(8,128)(2,1)}) %reduce-scatter.24.cloned.1.call-update) | async-done | bytes 131088 | tf_op jit(solution)/shard_map/reduce_scatter | solution.py:330
  1006.3 31.8 %reduce-scatter.38.cloned.1.call-done = bf16[2,512,256]{2,1,0:T(8,128)(2,1)} async-done(((bf16[2,512,1024]{2,1,0:T(8,128)(2,1)}), bf16[2,512,256]{2,1,0:T(8,128)(2,1)}) %reduce-scatter.38.cloned.1.call-update) | async-done | bytes 524304 | tf_op jit(solution)/shard_map/reduce_scatter | solution.py:366
  1040.2 29.7 %reduce-scatter.36.cloned.1.call-done = bf16[2,256,512]{2,1,0:T(8,128)(2,1)} async-done(((bf16[2,1024,512]{2,1,0:T(8,128)(2,1)}), bf16[2,256,512]{2,1,0:T(8,128)(2,1)}) %reduce-scatter.36.cloned.1.call-update) | async-done | bytes 524304 | tf_op jit(solution)/shard_map/reduce_scatter | solution.py:363
  1072.1 29.7 %reduce-scatter.34.cloned.1.call-done = bf16[2,256,512]{2,1,0:T(8,128)(2,1)} async-done(((bf16[2,1024,512]{2,1,0:T(8,128)(2,1)}), bf16[2,256,512]{2,1,0:T(8,128)(2,1)}) %reduce-scatter.34.cloned.1.call-update) | async-done | bytes 524304 | tf_op jit(solution)/shard_map/reduce_scatter | solution.py:360
  (758 shorter events, 220.2 us)
Async XLA Ops:
  7.2 174.7 %copy-start = (bf16[1,2,512,1024]{3,2,1,0:T(8,128)(2,1)S(1)}, bf16[1,2,512,1024]{3,2,1,0:T(8,128)(2,1)}, u32[]{:S(2)}) copy-start(bf16[1,2,512,1024]{3,2,1,0:T(8,128)(2,1)} %param.22) | copy-start | bytes 6291460
  7.2 17.4 %copy-start.208 = (bf16[1,64,128]{2,1,0:T(8,128)(2,1)S(1)}, bf16[1,64,128]{2,1,0:T(8,128)(2,1)}, u32[]{:S(2)}) copy-start(bf16[1,64,128]{2,1,0:T(8,128)(2,1)} %param.15) | copy-start | bytes 49156
  7.2 45.8 %copy-start.149 = (f32[1,1024]{1,0:T(1,128)S(1)}, f32[1,1024]{1,0:T(1,128)}, u32[]{:S(2)}) copy-start(f32[1,1024]{1,0:T(1,128)} %param.18) | copy-start | bytes 12292
  7.2 133.7 %reduce-scatter.14.cloned.1.call-start = ((), (), s32[]{:S(2)}) async-start(), calls=%async_computation.25 | async-start | bytes 655360 | tf_op jit(solution)/shard_map/reduce_scatter | solution.py:168
  10.4 43.4 %copy-start.187 = (bf16[1,64,256]{2,1,0:T(8,128)(2,1)S(1)}, bf16[1,64,256]{2,1,0:T(8,128)(2,1)}, u32[]{:S(2)}) copy-start(bf16[1,64,256]{2,1,0:T(8,128)(2,1)} %param.14) | copy-start | bytes 98308
  24.5 50.4 %copy-start.206 = (f32[256]{0:T(256)}, f32[256]{0:T(256)S(1)}, u32[]{:S(2)}) copy-start(f32[256]{0:T(256)S(1)} %fusion.111) | copy-start | bytes 3076
  24.6 71.8 %copy-start.217 = (f32[256]{0:T(256)}, f32[256]{0:T(256)S(1)}, u32[]{:S(2)}) copy-start(f32[256]{0:T(256)S(1)} %add_rsqrt_fusion.2) | copy-start | bytes 3076
  53.4 21.6 %copy-start.209 = (bf16[1,64,128]{2,1,0:T(8,128)(2,1)S(1)}, bf16[1,64,128]{2,1,0:T(8,128)(2,1)}, u32[]{:S(2)}) copy-start(bf16[1,64,128]{2,1,0:T(8,128)(2,1)} %param.16) | copy-start | bytes 49156
  74.5 21.9 %copy-start.27 = (bf16[1,1024,256]{2,1,0:T(8,128)(2,1)}, bf16[1,1024,256]{2,1,0:T(8,128)(2,1)S(1)}, u32[]{:S(2)}) copy-start(bf16[1,1024,256]{2,1,0:T(8,128)(2,1)S(1)} %all-gather.3) | copy-start | bytes 1572868
  74.5 22.3 %copy-start.188 = (bf16[1,64,256]{2,1,0:T(8,128)(2,1)S(1)}, bf16[1,64,256]{2,1,0:T(8,128)(2,1)}, u32[]{:S(2)}) copy-start(bf16[1,64,256]{2,1,0:T(8,128)(2,1)} %param.17) | copy-start | bytes 98308
  74.9 42.5 %copy-start.229 = (f32[256]{0:T(256)S(1)}, f32[256]{0:T(256)}, u32[]{:S(2)}) copy-start(f32[256]{0:T(256)} %subtract_convert_fusion.3) | copy-start | bytes 3076
  75.0 42.5 %copy-start.230 = (f32[256]{0:T(256)S(1)}, f32[256]{0:T(256)}, u32[]{:S(2)}) copy-start(f32[256]{0:T(256)} %subtract_convert_fusion.4) | copy-start | bytes 3076
  75.0 42.5 %copy-start.237 = (f32[32]{0:T(128)S(1)}, f32[32]{0:T(128)}, u32[]{:S(2)}) copy-start(f32[32]{0:T(128)} %negate_power_fusion) | copy-start | bytes 388
  96.3 23.2 %copy-start.59 = (bf16[1,1024,128]{2,1,0:T(8,128)(2,1)}, bf16[1,1024,128]{2,1,0:T(8,128)(2,1)S(1)}, u32[]{:S(2)}) copy-start(bf16[1,1024,128]{2,1,0:T(8,128)(2,1)S(1)} %all-gather.1) | copy-start | bytes 786436
  96.7 24.5 %copy-start.156 = (bf16[256,128]{0,1:T(8,128)(2,1)}, bf16[256,128]{0,1:T(8,128)(2,1)S(1)}, u32[]{:S(2)}) copy-start(bf16[256,128]{0,1:T(8,128)(2,1)S(1)} %convolution_convert_fusion.17) | copy-start | bytes 196612
  117.5 272.9 %copy-start.18 = (bf16[1,1024,256]{2,1,0:T(8,128)(2,1)}, bf16[1,1024,256]{2,1,0:T(8,128)(2,1)S(1)}, u32[]{:S(2)}) copy-start(bf16[1,1024,256]{2,1,0:T(8,128)(2,1)S(1)} %all-gather.4) | copy-start | bytes 1572868
  121.8 20.2 %copy-start.148 = (f32[1,1024]{1,0:T(1,128)S(1)}, f32[1,1024]{1,0:T(1,128)}, u32[]{:S(2)}) copy-start(f32[1,1024]{1,0:T(1,128)} %param.19) | copy-start | bytes 12292
  126.7 48.4 %copy-start.182 = (s32[64,8]{1,0:T(8,128)}, s32[64,8]{1,0:T(8,128)S(1)}, u32[]{:S(2)}) copy-start(s32[64,8]{1,0:T(8,128)S(1)} %bitcast_add_fusion.2) | copy-start | bytes 6148
  127.2 47.8 %copy-start.104 = (bf16[64,768]{1,0:T(8,128)(2,1)}, bf16[64,768]{1,0:T(8,128)(2,1)S(1)}, u32[]{:S(2)}) copy-start(bf16[64,768]{1,0:T(8,128)(2,1)S(1)} %fusion.131) | copy-start | bytes 294916
  141.9 33.1 %copy-start.224 = (f32[64]{0:T(128)}, f32[64]{0:T(128)S(1)}, u32[]{:S(2)}) copy-start(f32[64]{0:T(128)S(1)} %multiply_reduce_fusion.20) | copy-start | bytes 772
  185.6 28.5 %all-to-all-start.1 = ((bf16[2,384,1024]{2,0,1:T(2,128)(2,1)}), bf16[2,384,1024]{2,0,1:T(2,128)(2,1)}, u32[]{:S(2)}, u32[]{:S(2)}) async-start(bf16[2,384,1024]{2,0,1:T(2,128)(2,1)} %copy.212), calls=%async_computation.2 | async-start | bytes 3145728 | tf_op jit(solution)/shard_map/all_to_all | solution.py:187
  191.1 70.8 %reduce-scatter.16.cloned.1.call-start = ((), (), s32[]{:S(2)}) async-start(), calls=%async_computation.26 | async-start | bytes 655360 | tf_op jit(solution)/shard_map/reduce_scatter | solution.py:168
  191.6 24.4 %copy-start.197 = (s32[512]{0:T(512)}, s32[512]{0:T(512)S(1)}, u32[]{:S(2)}) copy-start(s32[512]{0:T(512)S(1)} %eq.265) | copy-start | bytes 6148
  217.5 14.9 %copy-start.207 = (f32[256]{0:T(256)S(1)}, f32[256]{0:T(256)}, u32[]{:S(2)}) copy-start(f32[256]{0:T(256)} %copy-done.206) | copy-start | bytes 3076
  217.5 15.5 %copy-start.55 = (bf16[1,1024,128]{2,1,0:T(8,128)(2,1)S(1)}, bf16[1,1024,128]{2,1,0:T(8,128)(2,1)}, u32[]{:S(2)}) copy-start(bf16[1,1024,128]{2,1,0:T(8,128)(2,1)} %copy-done.54) | copy-start | bytes 786436
  217.5 15.9 %copy-start.28 = (bf16[1,1024,256]{2,1,0:T(8,128)(2,1)S(1)}, bf16[1,1024,256]{2,1,0:T(8,128)(2,1)}, u32[]{:S(2)}) copy-start(bf16[1,1024,256]{2,1,0:T(8,128)(2,1)} %copy-done.27) | copy-start | bytes 1572868
  217.6 4.3 collective-permute-start
  234.5 158.4 %copy-start.44 = (bf16[256,2,2,64]{0,3,2,1:T(8,128)(2,1)}, bf16[256,2,2,64]{0,3,2,1:T(8,128)(2,1)S(1)}, u32[]{:S(2)}) copy-start(bf16[256,2,2,64]{0,3,2,1:T(8,128)(2,1)S(1)} %fusion.177) | copy-start | bytes 393220
  241.4 32.6 %all-to-all-start.4 = ((bf16[32,24,1024]{2,1,0:T(8,128)(2,1)}), bf16[32,24,1024]{2,1,0:T(8,128)(2,1)}, u32[]{:S(2)}, u32[]{:S(2)}) async-start(bf16[32,24,1024]{2,1,0:T(8,128)(2,1)} %bitcast.741), calls=%async_computation.6 | async-start | bytes 3145728 | tf_op jit(solution)/shard_map/all_to_all | solution.py:258
  274.0 28.6 %all-to-all-start.2 = ((bf16[32,24,1024]{2,1,0:T(8,128)(2,1)}), bf16[32,24,1024]{2,1,0:T(8,128)(2,1)}, u32[]{:S(2)}, u32[]{:S(2)}) async-start(bf16[32,24,1024]{2,1,0:T(8,128)(2,1)} %bitcast.722), calls=%async_computation.4 | async-start | bytes 3145728 | tf_op jit(solution)/shard_map/all_to_all | solution.py:180
  317.8 28.3 %all-to-all-start.5 = ((bf16[2,384,1024]{2,0,1:T(2,128)(2,1)}), bf16[2,384,1024]{2,0,1:T(2,128)(2,1)}, u32[]{:S(2)}, u32[]{:S(2)}) async-start(bf16[2,384,1024]{2,0,1:T(2,128)(2,1)} %copy.224), calls=%async_computation.7 | async-start | bytes 3145728 | tf_op jit(solution)/shard_map/all_to_all | solution.py:280
  346.1 28.2 %all-to-all-start.3 = ((bf16[2,384,1024]{2,0,1:T(2,128)(2,1)}), bf16[2,384,1024]{2,0,1:T(2,128)(2,1)}, u32[]{:S(2)}, u32[]{:S(2)}) async-start(bf16[2,384,1024]{2,0,1:T(2,128)(2,1)} %copy.219), calls=%async_computation.5 | async-start | bytes 3145728 | tf_op jit(solution)/shard_map/all_to_all | solution.py:187
  351.4 68.1 %reduce-scatter.18.cloned.1.call-start = ((), (), s32[]{:S(2)}) async-start(), calls=%async_computation.27 | async-start | bytes 655360 | tf_op jit(solution)/shard_map/reduce_scatter | solution.py:330
  379.4 11.3 %copy-start.154 = (bf16[256,128]{0,1:T(8,128)(2,1)S(1)}, bf16[256,128]{0,1:T(8,128)(2,1)}, u32[]{:S(2)}) copy-start(bf16[256,128]{0,1:T(8,128)(2,1)} %copy-done.153) | copy-start | bytes 196612
  379.4 11.3 %copy-start.157 = (bf16[256,128]{0,1:T(8,128)(2,1)S(1)}, bf16[256,128]{0,1:T(8,128)(2,1)}, u32[]{:S(2)}) copy-start(bf16[256,128]{0,1:T(8,128)(2,1)} %copy-done.156) | copy-start | bytes 196612
  397.2 29.1 %copy-start.101 = (bf16[1,2,1,64,1024]{4,3,2,1,0:T(8,128)(2,1)S(1)}, bf16[1,2,1,64,1024]{4,3,2,1,0:T(8,128)(2,1)}, u32[]{:S(2)}) copy-start(bf16[1,2,1,64,1024]{4,3,2,1,0:T(8,128)(2,1)} %param.13) | copy-start | bytes 786436
  397.3 72.8 %reduce-scatter.20.cloned.1.call-start = ((), (), s32[]{:S(2)}) async-start(), calls=%async_computation.28 | async-start | bytes 655360 | tf_op jit(solution)/shard_map/reduce_scatter | solution.py:168
  401.6 21.5 %collective-permute-start.1 = (bf16[64,1024]{1,0:T(8,128)(2,1)}, bf16[64,1024]{1,0:T(8,128)(2,1)S(1)}, u32[]{:S(2)}, u32[]{:S(2)}) collective-permute-start(bf16[64,1024]{1,0:T(8,128)(2,1)} %get-tuple-element.135), channel_id=1, source_target_pairs={{0,64},{1,65},{2,66},{3,67},{4,68},{5,69},{6,70},{7,71},{8,72},{9,... | collective-permute-start | bytes 393224 | tf_op jit(solution)/shard_map/ppermute | solution.py:18
  420.5 19.9 %copy-start.30 = (bf16[1,1024,256]{2,1,0:T(8,128)(2,1)S(1)}, bf16[1,1024,256]{2,1,0:T(8,128)(2,1)}, u32[]{:S(2)}) copy-start(bf16[1,1024,256]{2,1,0:T(8,128)(2,1)} %copy-done.27) | copy-start | bytes 1572868
  420.5 5.8 collective-permute-start.2
  448.4 36.1 %all-to-all-start.6 = ((bf16[32,24,1024]{2,1,0:T(8,128)(2,1)}), bf16[32,24,1024]{2,1,0:T(8,128)(2,1)}, u32[]{:S(2)}, u32[]{:S(2)}) async-start(bf16[32,24,1024]{2,1,0:T(8,128)(2,1)} %bitcast.739), calls=%async_computation.10 | async-start | bytes 3145728 | tf_op jit(solution)/shard_map/all_to_all | solution.py:258
  484.5 28.3 %all-to-all-start.7 = ((bf16[32,24,1024]{2,1,0:T(8,128)(2,1)}), bf16[32,24,1024]{2,1,0:T(8,128)(2,1)}, u32[]{:S(2)}, u32[]{:S(2)}) async-start(bf16[32,24,1024]{2,1,0:T(8,128)(2,1)} %bitcast.723), calls=%async_computation.11 | async-start | bytes 3145728 | tf_op jit(solution)/shard_map/all_to_all | solution.py:180
  526.7 28.2 %all-to-all-start.8 = ((bf16[2,384,1024]{2,0,1:T(2,128)(2,1)}), bf16[2,384,1024]{2,0,1:T(2,128)(2,1)}, u32[]{:S(2)}, u32[]{:S(2)}) async-start(bf16[2,384,1024]{2,0,1:T(2,128)(2,1)} %copy.236), calls=%async_computation.12 | async-start | bytes 3145728 | tf_op jit(solution)/shard_map/all_to_all | solution.py:280
  531.9 64.5 %reduce-scatter.22.cloned.1.call-start = ((), (), s32[]{:S(2)}) async-start(), calls=%async_computation.29 | async-start | bytes 655360 | tf_op jit(solution)/shard_map/reduce_scatter | solution.py:330
  558.4 11.3 %copy-start.158 = (bf16[256,128]{0,1:T(8,128)(2,1)S(1)}, bf16[256,128]{0,1:T(8,128)(2,1)}, u32[]{:S(2)}) copy-start(bf16[256,128]{0,1:T(8,128)(2,1)} %copy-done.156) | copy-start | bytes 196612
  558.4 11.3 %copy-start.164 = (bf16[256,128]{0,1:T(8,128)(2,1)S(1)}, bf16[256,128]{0,1:T(8,128)(2,1)}, u32[]{:S(2)}) copy-start(bf16[256,128]{0,1:T(8,128)(2,1)} %copy-done.163) | copy-start | bytes 196612
  598.1 6.0 collective-permute-start.3
  608.3 33.5 %all-to-all-start.9 = ((bf16[32,24,1024]{2,1,0:T(8,128)(2,1)}), bf16[32,24,1024]{2,1,0:T(8,128)(2,1)}, u32[]{:S(2)}, u32[]{:S(2)}) async-start(bf16[32,24,1024]{2,1,0:T(8,128)(2,1)} %bitcast.738), calls=%async_computation.14 | async-start | bytes 3145728 | tf_op jit(solution)/shard_map/all_to_all | solution.py:258
  654.9 28.3 %all-to-all-start.10 = ((bf16[2,384,1024]{2,0,1:T(2,128)(2,1)}), bf16[2,384,1024]{2,0,1:T(2,128)(2,1)}, u32[]{:S(2)}, u32[]{:S(2)}) async-start(bf16[2,384,1024]{2,0,1:T(2,128)(2,1)} %copy.244), calls=%async_computation.15 | async-start | bytes 3145728 | tf_op jit(solution)/shard_map/all_to_all | solution.py:280
  660.2 294.2 %reduce-scatter.30.cloned.1.call-start = ((), (), s32[]{:S(2)}) async-start(), calls=%async_computation.33 | async-start | bytes 278528 | tf_op jit(solution)/shard_map/reduce_scatter | solution.py:349
  687.2 11.5 %copy-start.155 = (bf16[256,128]{0,1:T(8,128)(2,1)S(1)}, bf16[256,128]{0,1:T(8,128)(2,1)}, u32[]{:S(2)}) copy-start(bf16[256,128]{0,1:T(8,128)(2,1)} %copy-done.153) | copy-start | bytes 196612
  687.2 11.5 %copy-start.165 = (bf16[256,128]{0,1:T(8,128)(2,1)S(1)}, bf16[256,128]{0,1:T(8,128)(2,1)}, u32[]{:S(2)}) copy-start(bf16[256,128]{0,1:T(8,128)(2,1)} %copy-done.163) | copy-start | bytes 196612
  704.4 251.4 %reduce-scatter.28.cloned.1.call-start = ((), (), s32[]{:S(2)}) async-start(), calls=%async_computation.32 | async-start | bytes 278528 | tf_op jit(solution)/shard_map/reduce_scatter | solution.py:346
  708.2 248.9 %reduce-scatter.32.cloned.1.call-start = ((), (), s32[]{:S(2)}) async-start(), calls=%async_computation.34 | async-start | bytes 557056 | tf_op jit(solution)/shard_map/reduce_scatter | solution.py:352
  712.6 268.6 %reduce-scatter.26.cloned.1.call-start = ((), (), s32[]{:S(2)}) async-start(), calls=%async_computation.31 | async-start | bytes 557056 | tf_op jit(solution)/shard_map/reduce_scatter | solution.py:343
  718.5 286.1 %reduce-scatter.24.cloned.1.call-start = ((), (), s32[]{:S(2)}) async-start(), calls=%async_computation.30 | async-start | bytes 655360 | tf_op jit(solution)/shard_map/reduce_scatter | solution.py:330
  722.1 316.0 %reduce-scatter.38.cloned.1.call-start = ((), (), s32[]{:S(2)}) async-start(), calls=%async_computation.37 | async-start | bytes 2621440 | tf_op jit(solution)/shard_map/reduce_scatter | solution.py:366
  729.0 341.0 %reduce-scatter.36.cloned.1.call-start = ((), (), s32[]{:S(2)}) async-start(), calls=%async_computation.36 | async-start | bytes 2621440 | tf_op jit(solution)/shard_map/reduce_scatter | solution.py:363
  737.5 364.2 %reduce-scatter.34.cloned.1.call-start = ((), (), s32[]{:S(2)}) async-start(), calls=%async_computation.35 | async-start | bytes 2621440 | tf_op jit(solution)/shard_map/reduce_scatter | solution.py:360
  751.1 31.9 %all-to-all-start.11 = ((bf16[2,384,1024]{2,0,1:T(2,128)(2,1)}), bf16[2,384,1024]{2,0,1:T(2,128)(2,1)}, u32[]{:S(2)}, u32[]{:S(2)}) async-start(bf16[2,384,1024]{2,0,1:T(2,128)(2,1)} %copy.250), calls=%async_computation.17 | async-start | bytes 3145728 | tf_op jit(solution)/shard_map/all_to_all | solution.py:187
  783.0 168.5 %copy-start.179 = (s32[64,8]{1,0:T(8,128)S(1)}, s32[64,8]{1,0:T(8,128)}, u32[]{:S(2)}) copy-start(s32[64,8]{1,0:T(8,128)} %copy-done.178) | copy-start | bytes 6148
  951.5 53.1 %copy-start.70 = (bf16[64,1024]{1,0:T(8,128)(2,1)S(1)}, bf16[64,1024]{1,0:T(8,128)(2,1)}, u32[]{:S(2)}) copy-start(bf16[64,1024]{1,0:T(8,128)(2,1)} %reduce-scatter.20.cloned.1.call-done) | copy-start | bytes 393220
  951.5 53.1 %copy-start.131 = (f32[64,1024]{1,0:T(8,128)S(1)}, f32[64,1024]{1,0:T(8,128)}, u32[]{:S(2)}) copy-start(f32[64,1024]{1,0:T(8,128)} %get-tuple-element.89) | copy-start | bytes 786436
  951.5 54.1 %copy-start.147 = (bf16[1,64,1024]{2,1,0:T(8,128)(2,1)S(1)}, bf16[1,64,1024]{2,1,0:T(8,128)(2,1)}, u32[]{:S(2)}) copy-start(bf16[1,64,1024]{2,1,0:T(8,128)(2,1)} %get-tuple-element.80) | copy-start | bytes 393220
  (204 other events, 550.4 us)
Sparse Core Ops, SparseCore 0:
  123.7 17.1 reduce-scatter.13
  238.1 23.7 reduce-scatter.15
  397.4 22.0 reduce-scatter.17
  445.1 24.9 reduce-scatter.19
  575.7 20.6 reduce-scatter.21
  704.5 66.1 reduce-scatter.29
  774.3 69.2 reduce-scatter.27
  847.3 64.5 reduce-scatter.31
  916.7 64.5 reduce-scatter.25
  984.1 20.4 reduce-scatter.23
  1007.0 31.1 reduce-scatter.37
  1040.5 29.3 reduce-scatter.35
  1072.3 29.3 reduce-scatter.33
where the time goes:
time: 1120 us; the launch traced here: 1110 us
  waiting for transfers between devices  384 us (34%)
  blocking collectives  351 us (31%)
  matrix products  122 us (11%)
  starting transfers between devices  90.2 us (8%)
  local copies, waits for them, and re-layouts  85.2 us (8%)
  other arithmetic  60.8 us (5%)
  between operations  17.4 us (2%)
    psum x1, blocking collectives, sum_gains(): return lax.psum((grads_two[0], grads_two[1]), ('row', 'col'))  165 us
    all_to_all x3, waiting for transfers between devices, layer_forward(): lax.all_to_all(produced, 'col', split_axis=1, concat_axis=0, tiled=True)  58.1 us
    reduce_scatter x3, waiting for transfers between devices, layer_backward(): lax.psum_scatter(grad_packed.astype(jnp.bfloat16), 'row', scatter_dimensi...  56.8 us
    all_to_all x3, waiting for transfers between devices, layer_backward(): lax.all_to_all(grad_arrived.astype(jnp.bfloat16), 'col', split_axis=1, co...  54 us
    all_to_all x2, waiting for transfers between devices, layer_forward(): lax.all_to_all(sending, 'col', split_axis=0, concat_axis=1, tiled=True)  40.3 us
    dot_general x18, matrix products, contract_rows(): lax.dot_general(left_mat, right_mat, (((0,), (0,)), ((), ())), preferred_...  35.5 us
    all_to_all x3, starting transfers between devices, layer_backward(): lax.all_to_all(grad_back, 'col', split_axis=0, concat_axis=1, tiled=True)  33.6 us
    all_gather x3, blocking collectives, layer_forward(): packed = lax.all_gather(quarter_rows, 'row', axis=0, tiled=True)  33 us
  transfers between devices with their start and end apart: 28, of which 24 were waited for; matrix products, arithmetic and copies ran while one was open for 12% of the time, Pallas kernels for 0%

commit v1 on v0

v1 whole, which is shorter than its diff:
```python
import functools

import jax
import jax.numpy as jnp
from jax import lax
from jax.experimental import pallas as pl
from jax.experimental.pallas import tpu as pltpu
from jax.sharding import PartitionSpec as P

D = 1024
FF = 512
HEAD = 64
TOK = 64
ROWS = 4
COLS = 16
CHIPS = 8
CAP = 24
PACK = 256
SLOTS = COLS * CAP
QUADS = 4

SCORE_MUL = 0.015625
RESID_MUL = 0.22
NORM_EPS = 1e-06
ROPE_THETA = 10000.0
MESH = pl.DeviceIdType.MESH
BF = jnp.bfloat16
F32 = jnp.float32
VM = pl.BlockSpec(memory_space=pltpu.VMEM)
DMA = pltpu.SemaphoreType.DMA


def dot(a, b):
    return jnp.dot(a, b, preferred_element_type=F32)


def dot_rows(a, b):
    return lax.dot_general(a, b, (((0,), (0,)), ((), ())), preferred_element_type=F32)


def dot_cols(a, b):
    return lax.dot_general(a, b, (((1,), (1,)), ((), ())), preferred_element_type=F32)


class Place:
    def __init__(self):
        self.section = lax.axis_index("section")
        self.row = lax.axis_index("row")
        self.col = lax.axis_index("col")
        self.chip = self.col // 2
        self.core = lax.rem(self.col, 2)

    def row_peer(self, step):
        return (self.section, lax.rem(self.row + step, ROWS), self.col)

    def chip_at(self, step):
        return lax.rem(self.chip + step + CHIPS, CHIPS)

    def chip_peer(self, step):
        return (self.section, self.row, self.chip_at(step) * 2 + self.core)

    def buddy(self):
        return (self.section, self.row, self.chip * 2 + 1 - self.core)

    def across(self):
        return (1 - self.section, self.row, self.col)


def greet(partners):
    barrier = pltpu.get_barrier_semaphore()
    for partner in partners:
        pl.semaphore_signal(barrier, inc=1, device_id=partner, device_id_type=MESH)
    pl.semaphore_wait(barrier, len(partners))


def remote(src, dst, send, recv, device):
    return pltpu.make_async_remote_copy(
        src_ref=src, dst_ref=dst, send_sem=send, recv_sem=recv, device_id=device, device_id_type=MESH
    )


def row_partners(me):
    return [me.row_peer(step) for step in (1, 2, 3)]


def col_partners(me):
    return [me.chip_peer(step) for step in range(1, CHIPS)] + [me.buddy()]


ROW_SEMS = [DMA((3,)), DMA((3,))]
COL_SEMS = [DMA((7,)), DMA((7,)), DMA((8,)), DMA((8,))]


def gather_row_start(me, out, sems):
    copies = []
    for step in (2, 1, 3):
        copy = remote(
            out.at[me.row], out.at[me.row], sems[0].at[step - 1], sems[1].at[step - 1], me.row_peer(step)
        )
        copy.start()
        copies.append(copy)
    return copies


def gather_row_finish(me, out, sems, copies):
    for step in (1, 3, 2):
        origin = lax.rem(me.row - step + ROWS, ROWS)
        remote(
            out.at[origin], out.at[origin], sems[0].at[step - 1], sems[1].at[step - 1], me.row_peer(step)
        ).wait_recv()
    for copy in copies:
        copy.wait_send()


def gather_col_start(me, out, sems):
    copies = []
    for step in (4, 2, 6, 5, 3, 7, 1):
        copy = remote(
            out.at[me.col], out.at[me.col], sems[0].at[step - 1], sems[1].at[step - 1], me.chip_peer(step)
        )
        copy.start()
        copies.append(copy)
    copy = remote(out.at[me.col], out.at[me.col], sems[2].at[0], sems[3].at[0], me.buddy())
    copy.start()
    copies.append(copy)
    return copies


def gather_col_finish(me, out, sems, copies):
    for step in (1, 7, 3, 5, 2, 6, 4):
        origin = me.chip_at(-step) * 2 + me.core
        remote(
            out.at[origin], out.at[origin], sems[0].at[step - 1], sems[1].at[step - 1], me.chip_peer(step)
        ).wait_recv()
        copy = remote(out.at[origin], out.at[origin], sems[2].at[step], sems[3].at[step], me.buddy())
        copy.start()
        copies.append(copy)
    for step in range(CHIPS):
        origin = me.chip_at(-step) * 2 + 1 - me.core
        remote(
            out.at[origin], out.at[origin], sems[2].at[step], sems[3].at[step], me.buddy()
        ).wait_recv()
    for copy in copies:
        copy.wait_send()


def sum_row(me, part, landing, sems):
    copies = []
    for step in (2, 1, 3):
        target = lax.rem(me.row + step, ROWS)
        copy = remote(
            part.at[target], landing.at[step - 1], sems[0].at[step - 1], sems[1].at[step - 1], me.row_peer(step)
        )
        copy.start()
        copies.append((step, copy))
    total = part[me.row].astype(F32)
    for step, copy in copies[1:] + copies[:1]:
        copy.wait_recv()
        total = total + landing[step - 1].astype(F32)
    return total, [copy for _, copy in copies]


SUM_STEPS = (4, 2, 6, 5, 3, 7, 1)


def sum_col(me, part, halves, outgoing, landing, sems):
    first = []
    for step in SUM_STEPS + (0,):
        target = me.chip_at(step) * 2 + 1 - me.core
        copy = remote(part.at[target], halves.at[step], sems[2].at[step], sems[3].at[step], me.buddy())
        copy.start()
        first.append(copy)
    second = []
    for step, copy in zip(SUM_STEPS, first):
        copy.wait_recv()
        mine = me.chip_at(step) * 2 + me.core
        outgoing[step - 1] = (part[mine].astype(F32) + halves[step].astype(F32)).astype(BF)
        away = remote(
            outgoing.at[step - 1], landing.at[step - 1], sems[0].at[step - 1], sems[1].at[step - 1], me.chip_peer(step)
        )
        away.start()
        second.append(away)
    first[-1].wait_recv()
    total = part[me.col].astype(F32) + halves[0].astype(F32)
    for step, away in list(zip(SUM_STEPS, second))[::-1]:
        away.wait_recv()
        total = total + landing[step - 1].astype(F32)
    return total, first + second


def finish(copies):
    for copy in copies:
        copy.wait_send()


def sum_col_scratch(width):
    return [
        pltpu.VMEM((8, TOK, width), BF),
        pltpu.VMEM((7, TOK, width), BF),
        pltpu.VMEM((7, TOK, width), BF),
    ]


def start_kernel(w_ref, rg_ref, x_ref, w_out, rg_out, x_out, *sems):
    me = Place()
    greet(row_partners(me) + col_partners(me))
    w_out[me.col] = w_ref[...]
    rg_out[me.col] = rg_ref[...]
    x_out[me.row] = x_ref[...]
    xs = gather_row_start(me, x_out, sems[0:2])
    rs = gather_col_start(me, rg_out, sems[2:6])
    ws = gather_col_start(me, w_out, sems[6:10])
    gather_row_finish(me, x_out, sems[0:2], xs)
    gather_col_finish(me, rg_out, sems[2:6], rs)
    gather_col_finish(me, w_out, sems[6:10], ws)


def attended_kernel(part, packed, gain, resid, out, landing, *sems):
    me = Place()
    greet(row_partners(me) + col_partners(me))
    total, copies = sum_row(me, part, landing, sems[0:2])
    value = packed[me.row].astype(F32) + RESID_MUL * total
    resid[...] = value
    scale = lax.rsqrt(jnp.mean(value * value, axis=1, keepdims=True) + NORM_EPS)
    out[me.col] = (value * scale * gain[...]).astype(BF)
    gathers = gather_col_start(me, out, sems[2:6])
    finish(copies)
    gather_col_finish(me, out, sems[2:6], gathers)


def mixed_kernel(part, resid, coming, nexth, out, arrived, halves, outgoing, landing, *sems):
    me = Place()
    greet(row_partners(me) + col_partners(me) + [me.across()])
    total, copies = sum_col(me, part, halves, outgoing, landing, sems[2:6])
    nexth[...] = (resid[...] + RESID_MUL * total).astype(BF)
    over = remote(nexth, arrived, sems[6].at[0], sems[7].at[0], me.across())
    over.start()
    over.wait_recv()
    out[me.row] = jnp.where(me.section == 0, coming[...], arrived[...])
    gathers = gather_row_start(me, out, sems[0:2])
    finish(copies)
    over.wait_send()
    gather_row_finish(me, out, sems[0:2], gathers)


def last_mixed_kernel(part, resid, coming, nexth, out, halves, outgoing, landing, *sems):
    me = Place()
    greet(col_partners(me))
    total, copies = sum_col(me, part, halves, outgoing, landing, sems[0:4])
    out[me.col] = coming[...]
    gathers = gather_col_start(me, out, sems[4:8])
    nexth[...] = (resid[...] + RESID_MUL * total).astype(BF)
    finish(copies)
    gather_col_finish(me, out, sems[4:8], gathers)


def normed_back_kernel(part, resid, entry, gain, dr, dgain, out, halves, outgoing, landing, *sems):
    me = Place()
    greet(row_partners(me) + col_partners(me))
    total, copies = sum_col(me, part, halves, outgoing, landing, sems[2:6])
    value = resid[...]
    scale = lax.rsqrt(jnp.mean(value * value, axis=1, keepdims=True) + NORM_EPS)
    weighted = total * gain[...]
    inner = jnp.mean(weighted * value, axis=1, keepdims=True)
    grad = entry[...].astype(F32) + scale * weighted - value * (scale * scale * scale) * inner
    out[me.row] = (RESID_MUL * grad).astype(BF)
    gathers = gather_row_start(me, out, sems[0:2])
    dr[...] = grad
    dgain[...] = jnp.sum(total * value * scale, axis=0, keepdims=True)
    finish(copies)
    gather_row_finish(me, out, sems[0:2], gathers)


def input_back_kernel(part, dr, coming, dhin, entry, out, arrived, landing, *sems):
    me = Place()
    greet(row_partners(me) + col_partners(me) + [me.across()])
    total, copies = sum_row(me, part, landing, sems[0:2])
    dhin[...] = (total + dr[...]).astype(BF)
    over = remote(dhin, arrived, sems[6].at[0], sems[7].at[0], me.across())
    over.start()
    over.wait_recv()
    chosen = jnp.where(me.section == 0, arrived[...], coming[...])
    entry[...] = chosen
    out[me.col] = chosen
    gathers = gather_col_start(me, out, sems[2:6])
    finish(copies)
    over.wait_send()
    gather_col_finish(me, out, sems[2:6], gathers)


def last_back_kernel(part, dr, dhin, landing, *sems):
    me = Place()
    greet(row_partners(me))
    total, copies = sum_row(me, part, landing, sems[0:2])
    dhin[...] = (total + dr[...]).astype(BF)
    finish(copies)


def weights_sum_kernel(part, gains, out, gains_out, halves, outgoing, landing, g_one, g_two, g_three, *sems):
    me = Place()
    greet(row_partners(me) + col_partners(me))
    near = remote(gains, g_one, sems[6].at[0], sems[7].at[0], me.buddy())
    near.start()
    total, copies = sum_col(me, part, halves, outgoing, landing, sems[2:6])
    near.wait_recv()
    g_two[7] = gains[...] + g_one[...]
    chips = []
    for step in range(1, CHIPS):
        copy = remote(g_two.at[7], g_two.at[step - 1], sems[6].at[step], sems[7].at[step], me.chip_peer(step))
        copy.start()
        chips.append(copy)
    out[...] = total
    for copy in chips:
        copy.wait_recv()
    g_three[3] = jnp.sum(g_two[...], axis=0)
    rows = []
    for step in (1, 2, 3):
        copy = remote(g_three.at[3], g_three.at[step - 1], sems[0].at[step - 1], sems[1].at[step - 1], me.row_peer(step))
        copy.start()
        rows.append(copy)
    for copy in rows:
        copy.wait_recv()
    gains_out[...] = (g_three[3] + g_three[0]) + (g_three[1] + g_three[2])
    finish(copies + chips + rows + [near])


def call_remote(kernel, ident, outs, scratch, *args):
    return pl.pallas_call(
        kernel,
        out_shape=outs,
        in_specs=[VM] * len(args),
        out_specs=[VM] * len(outs),
        scratch_shapes=scratch,
        compiler_params=pltpu.CompilerParams(
            collective_id=ident, has_side_effects=True, vmem_limit_bytes=48 * 2**20
        ),
        cost_estimate=pl.CostEstimate(flops=10**6, bytes_accessed=40 * 10**6, transcendentals=0),
    )(*args)


def sds(shape, kind):
    return jax.ShapeDtypeStruct(shape, kind)


ACROSS = [DMA((1,)), DMA((1,))]
LAND_ROW = [pltpu.VMEM((3, TOK, D), BF)]
ARRIVED = [pltpu.VMEM((TOK, D), BF)]


def run_start(w, rg, x):
    return call_remote(
        start_kernel, 0,
        [sds((COLS,) + w.shape, BF), sds((COLS,) + rg.shape, F32), sds((ROWS, TOK, D), BF)],
        ROW_SEMS + COL_SEMS + COL_SEMS, w, rg, x,
    )


def run_attended(part, packed, gain):
    return call_remote(
        attended_kernel, 1, [sds((TOK, D), F32), sds((COLS, TOK, D), BF)],
        LAND_ROW + ROW_SEMS + COL_SEMS, part, packed, gain,
    )


def run_mixed(part, resid, coming):
    return call_remote(
        mixed_kernel, 2, [sds((TOK, D), BF), sds((ROWS, TOK, D), BF)],
        ARRIVED + sum_col_scratch(D) + ROW_SEMS + COL_SEMS + ACROSS, part, resid, coming,
    )


def run_last_mixed(part, resid, coming):
    return call_remote(
        last_mixed_kernel, 3, [sds((TOK, D), BF), sds((COLS, TOK, D), BF)],
        sum_col_scratch(D) + COL_SEMS + COL_SEMS, part, resid, coming,
    )


def run_normed_back(part, resid, entry, gain):
    return call_remote(
        normed_back_kernel, 4, [sds((TOK, D), F32), sds((1, D), F32), sds((ROWS, TOK, D), BF)],
        sum_col_scratch(D) + ROW_SEMS + COL_SEMS, part, resid, entry, gain,
    )


def run_input_back(part, dr, coming):
    return call_remote(
        input_back_kernel, 5, [sds((TOK, D), BF), sds((TOK, D), BF), sds((COLS, TOK, D), BF)],
        ARRIVED + LAND_ROW + ROW_SEMS + COL_SEMS + ACROSS, part, dr, coming,
    )


def run_last_back(part, dr):
    return call_remote(last_back_kernel, 6, [sds((TOK, D), BF)], LAND_ROW + ROW_SEMS, part, dr)[0]


def run_weights_sum(part, gains):
    width = part.shape[-1]
    return call_remote(
        weights_sum_kernel, 7, [sds((TOK, width), F32), sds((2, D), F32)],
        sum_col_scratch(width)
        + [pltpu.VMEM((2, D), F32), pltpu.VMEM((8, 2, D), F32), pltpu.VMEM((4, 2, D), F32)]
        + ROW_SEMS + COL_SEMS + [DMA((8,)), DMA((8,))],
        part, gains,
    )


def swap_halves(value):
    width = value.shape[1]
    lane = lax.broadcasted_iota(jnp.int32, value.shape, 1)
    low = lax.rem(lane, HEAD) < HEAD // 2
    up = pltpu.roll(value, HEAD // 2, axis=1)
    down = pltpu.roll(value, width - HEAD // 2, axis=1)
    return low, up, down


def rope(value, cosine, sine):
    low, up, down = swap_halves(value)
    return value * cosine + jnp.where(low, -down, up) * sine


def rope_back(value, cosine, sine):
    low, up, down = swap_halves(value * sine)
    return value * cosine + jnp.where(low, down, -up)


def allowed_mask(seg, seg_t):
    shape = (PACK, PACK)
    query = lax.broadcasted_iota(jnp.int32, shape, 0)
    key = lax.broadcasted_iota(jnp.int32, shape, 1)
    return (seg[...] == seg_t[...]) & (key <= query)


def probabilities(q, k, allowed):
    scores = jnp.where(allowed, dot_cols(q, k) * SCORE_MUL, -1e30)
    weights = jnp.exp(scores - jnp.max(scores, axis=1, keepdims=True))
    return weights / jnp.sum(weights, axis=1, keepdims=True)


def attention_kernel(x_ref, w, gain, cosine, sine, seg, seg_t, part, n1, q_out, kv_out, o_out):
    x = x_ref[...].astype(F32)
    scale = lax.rsqrt(jnp.mean(x * x, axis=1, keepdims=True) + NORM_EPS)
    normed = (x * scale * gain[...]).astype(BF)
    n1[...] = normed
    cos, sin = cosine[...], sine[...]
    pre = dot(normed, w[:, 0:512])
    q = jnp.concatenate(
        [rope(pre[:, 0:128], cos, sin), rope(pre[:, 128:256], cos, sin)], axis=1
    ).astype(BF)
    k = rope(pre[:, 256:384], cos, sin).astype(BF)
    v = pre[:, 384:512].astype(BF)
    q_out[...] = q
    kv_out[:, 0:128] = k
    kv_out[:, 128:256] = v
    allowed = allowed_mask(seg, seg_t)
    heads = []
    for head in range(4):
        at = (head // 2) * HEAD
        prob = probabilities(q[:, head * HEAD:(head + 1) * HEAD], k[:, at:at + HEAD], allowed)
        heads.append(dot(prob.astype(BF), v[:, at:at + HEAD]))
    mixed = jnp.concatenate(heads, axis=1).astype(BF)
    o_out[...] = mixed
    part[...] = dot_cols(mixed, w[:, 512:768]).astype(BF)


def attention_back_kernel(
    da, x_ref, w, gain, cosine, sine, seg, seg_t, q_ref, kv_ref, part, dp_out, dgain
):
    cos, sin = cosine[...], sine[...]
    do = dot(da[...], w[:, 512:768]).astype(BF)
    q = q_ref[...]
    kv = kv_ref[...]
    allowed = allowed_mask(seg, seg_t)
    dqs, dks, dvs = [], [None, None], [None, None]
    for head in range(4):
        group = head // 2
        at = group * HEAD
        qh = q[:, head * HEAD:(head + 1) * HEAD]
        kh = kv[:, at:at + HEAD]
        vh = kv[:, 128 + at:128 + at + HEAD]
        doh = do[:, head * HEAD:(head + 1) * HEAD]
        prob = probabilities(qh, kh, allowed)
        dv = dot_rows(prob.astype(BF), doh)
        dprob = dot_cols(doh, vh)
        ds = (prob * (dprob - jnp.sum(prob * dprob, axis=1, keepdims=True))).astype(BF)
        dqs.append(dot(ds, kh) * SCORE_MUL)
        dk = dot_rows(ds, qh) * SCORE_MUL
        dks[group] = dk if dks[group] is None else dks[group] + dk
        dvs[group] = dv if dvs[group] is None else dvs[group] + dv
    dp = jnp.concatenate(
        [
            rope_back(jnp.concatenate(dqs[0:2], axis=1), cos, sin),
            rope_back(jnp.concatenate(dqs[2:4], axis=1), cos, sin),
            rope_back(jnp.concatenate(dks, axis=1), cos, sin),
            jnp.concatenate(dvs, axis=1),
        ],
        axis=1,
    ).astype(BF)
    dp_out[...] = dp
    dn1 = dot_cols(dp, w[:, 0:512])
    x = x_ref[...].astype(F32)
    scale = lax.rsqrt(jnp.mean(x * x, axis=1, keepdims=True) + NORM_EPS)
    dgain[...] = jnp.sum(dn1 * x * scale, axis=0, keepdims=True)
    weighted = dn1 * gain[...]
    inner = jnp.mean(weighted * x, axis=1, keepdims=True)
    part[...] = (scale * weighted - x * (scale * scale * scale) * inner).astype(BF)


def place_rows(table, rows, out):
    for quad in range(QUADS):
        out[quad * 96:(quad + 1) * 96, :] = dot(
            table[0, quad], rows[quad * 256:(quad + 1) * 256, :]
        ).astype(out.dtype)


def return_rows(table, rows, acc, out):
    expert = pl.program_id(0)
    for quad in range(QUADS):
        span = pl.ds(quad * 256, 256)
        value = dot_rows(table[0, quad], rows[quad * 96:(quad + 1) * 96, :])

        @pl.when(expert == 0)
        def _():
            acc[span, :] = value

        @pl.when(expert == 1)
        def _():
            out[span, :] = (acc[span, :] + value).astype(BF)


def experts_kernel(rows, table, gslot, wg, wu, wd, part, xs, g_out, u_out, acc):
    place_rows(table, rows, xs.at[0])
    x = xs[0]
    g = dot(x, wg[0])
    u = dot(x, wu[0])
    g_out[0] = g
    u_out[0] = u
    z = (g * jax.nn.sigmoid(g) * u).astype(BF)
    y = dot(z, wd[0]).astype(BF).astype(F32)
    y = (y * gslot[0]).astype(BF)
    return_rows(table, y, acc, part)


def experts_back_kernel(
    rows, table, gslot, g_ref, u_ref, wg, wu, wd, part, dy_out, dg_out, du_out, z_out, acc, dy_raw
):
    place_rows(table, rows, dy_raw)
    dy = ((RESID_MUL * gslot[0]) * dy_raw[...]).astype(BF)
    dy_out[0] = dy
    dz = dot_cols(dy, wd[0])
    g, u = g_ref[0], u_ref[0]
    sig = jax.nn.sigmoid(g)
    silu = g * sig
    z_out[0] = (silu * u).astype(BF)
    dg = (dz * u * sig * (1.0 + g * (1.0 - sig))).astype(BF)
    du = (dz * silu).astype(BF)
    dg_out[0] = dg
    du_out[0] = du
    dx = (dot_cols(dg, wg[0]) + dot_cols(du, wu[0])).astype(BF)
    return_rows(table, dx, acc, part)


def expert_weights_kernel(xa, xb, ga, gb, ua, ub, za, zb, ya, yb, out):
    for j in range(ROWS):
        span = slice(j * 256, (j + 1) * 256)
        left_a, left_b = xa[0, :, span], xb[0, :, span]
        out[j, 0, 0] = (dot_rows(left_a, ga[0]) + dot_rows(left_b, gb[0])).astype(BF)
        out[j, 1, 0] = (dot_rows(left_a, ua[0]) + dot_rows(left_b, ub[0])).astype(BF)
        out[j, 2, 0] = (dot_rows(ya[0, :, span], za[0]) + dot_rows(yb[0, :, span], zb[0])).astype(BF)


def attention_weights_kernel(na, nb, pa, pb, da_a, da_b, oa, ob, out):
    out[:, 0:512] = (dot_rows(na[...], pa[...]) + dot_rows(nb[...], pb[...])).astype(BF)
    out[:, 512:768] = (dot_rows(da_a[...], oa[...]) + dot_rows(da_b[...], ob[...])).astype(BF)


def call_local(kernel, outs, flops, *args):
    return pl.pallas_call(
        kernel,
        out_shape=outs,
        in_specs=[VM] * len(args),
        out_specs=[VM] * len(outs),
        compiler_params=pltpu.CompilerParams(vmem_limit_bytes=48 * 2**20),
        cost_estimate=pl.CostEstimate(flops=flops, bytes_accessed=6 * 10**6, transcendentals=0),
    )(*args)


def call_experts(kernel, outs, scratch, flops, args, whole):
    def spec(shape, constant):
        if constant:
            return pl.BlockSpec(shape, lambda e: (0,) * len(shape))
        return pl.BlockSpec((1,) + shape[1:], lambda e: (e,) + (0,) * (len(shape) - 1))

    return pl.pallas_call(
        kernel,
        grid=(2,),
        out_shape=[shape for shape, _ in outs],
        in_specs=[spec(a.shape, c) for a, c in zip(args, whole)],
        out_specs=[spec(shape.shape, c) for shape, c in outs],
        scratch_shapes=scratch,
        compiler_params=pltpu.CompilerParams(
            vmem_limit_bytes=56 * 2**20, dimension_semantics=("arbitrary",)
        ),
        cost_estimate=pl.CostEstimate(flops=flops, bytes_accessed=20 * 10**6, transcendentals=0),
    )(*args)


def run_attention(packed, w, gain, tables):
    return call_local(
        attention_kernel,
        [sds((PACK, D), BF), sds((PACK, D), BF), sds((PACK, 256), BF), sds((PACK, 256), BF), sds((PACK, 256), BF)],
        10**9, packed, w, gain, *tables,
    )


def run_attention_back(da, packed, w, gain, tables, q, kv):
    return call_local(
        attention_back_kernel,
        [sds((PACK, D), BF), sds((PACK, 512), BF), sds((1, D), F32)],
        10**9, da, packed, w, gain, *tables, q, kv,
    )


def run_experts(rows, routing, mats):
    table, gslot = routing
    ff = sds((2, SLOTS, FF), F32)
    return call_experts(
        experts_kernel,
        [(sds((D, D), BF), True), (sds((2, SLOTS, D), BF), False), (ff, False), (ff, False)],
        [pltpu.VMEM((D, D), F32)],
        4 * 10**9,
        (rows, table, gslot) + mats,
        (True, False, False, False, False, False),
    )


def run_experts_back(rows, routing, g, u, mats):
    table, gslot = routing
    ff = sds((2, SLOTS, FF), BF)
    return call_experts(
        experts_back_kernel,
        [(sds((D, D), BF), True), (sds((2, SLOTS, D), BF), False), (ff, False), (ff, False), (ff, False)],
        [pltpu.VMEM((D, D), F32), pltpu.VMEM((SLOTS, D), F32)],
        4 * 10**9,
        (rows, table, gslot, g, u) + mats,
        (True,) + (False,) * 7,
    )


def run_expert_weights(*pairs):
    args = [item for pair in pairs for item in pair]
    out = sds((ROWS, 3, 2, 256, FF), BF)

    def spec(shape):
        return pl.BlockSpec((1,) + shape[1:], lambda e: (e, 0, 0))

    return pl.pallas_call(
        expert_weights_kernel,
        grid=(2,),
        out_shape=out,
        in_specs=[spec(a.shape) for a in args],
        out_specs=pl.BlockSpec((ROWS, 3, 1, 256, FF), lambda e: (0, 0, e, 0, 0)),
        compiler_params=pltpu.CompilerParams(
            vmem_limit_bytes=56 * 2**20, dimension_semantics=("arbitrary",)
        ),
        cost_estimate=pl.CostEstimate(flops=5 * 10**9, bytes_accessed=20 * 10**6, transcendentals=0),
    )(*args)


def layout_tables(length_row):
    ends_at = jnp.cumsum(length_row)
    places = jnp.arange(PACK, dtype=jnp.int32)
    passed = places[:, None] >= ends_at[None, :]
    segment = jnp.sum(passed.astype(jnp.int32), axis=1)
    starts = jnp.sum(jnp.where(passed, length_row[None, :], 0), axis=1)
    offset = (places - starts).astype(F32)
    frequency = ROPE_THETA ** (-(jnp.arange(HEAD // 2, dtype=F32) * 2.0 / HEAD))
    angles = offset[:, None] * frequency[None, :]
    cosine = jnp.tile(jnp.cos(angles), (1, 4))
    sine = jnp.tile(jnp.sin(angles), (1, 4))
    return (cosine, sine, segment[:, None], segment[None, :])


def routing_tables(route_all, gate_all, col):
    mine = col * 2 + jnp.arange(2, dtype=jnp.int32)
    same = route_all[None] == mine[:, None, None, None]
    chosen = jnp.any(same, axis=3)
    gate = jnp.sum(jnp.where(same, gate_all[None], 0.0), axis=3)
    before = (jnp.arange(TOK)[:, None] < jnp.arange(TOK)[None, :]).astype(BF)
    rank = jnp.einsum("est,tu->esu", chosen.astype(BF), before, preferred_element_type=F32)
    slot = jnp.where(chosen, rank, -1.0)
    onehot = slot[:, :, None, :] == jnp.arange(CAP, dtype=F32)[None, None, :, None]
    gslot = jnp.sum(jnp.where(onehot, gate[:, :, None, :], 0.0), axis=3)
    blocks = onehot.reshape(2, QUADS, 4, CAP, 1, TOK)
    diagonal = jnp.eye(4, dtype=jnp.bool_).reshape(1, 1, 4, 1, 4, 1)
    table = (blocks & diagonal).astype(BF).reshape(2, QUADS, 4 * CAP, 4 * TOK)
    return (table, gslot.reshape(2, SLOTS, 1))


def per_device(
    ends_in, q_weight, key_projection, value_projection, out_weight, attn_gain, moe_gain,
    gate_weight, up_weight, down_weight, routes, gates, lengths,
):
    section = lax.axis_index("section")
    col = lax.axis_index("col")
    ends = ends_in[0, :, 0]
    own = jnp.concatenate([q_weight[0], key_projection[0], value_projection[0], out_weight[0]], axis=1)
    mine = jnp.concatenate([routes[0, :, 0].astype(F32).reshape(8, 128), gates[0, :, 0].reshape(8, 128)], axis=0)
    weights, shared, packed0 = run_start(own, mine, ends[0])
    weights = weights.reshape(D, 768)
    route_all = shared[:, 0:8].reshape(COLS, 2, TOK, 8).astype(jnp.int32)
    gate_all = shared[:, 8:16].reshape(COLS, 2, TOK, 8)
    mats = (gate_weight[0], up_weight[0], down_weight[0])
    attn_row, moe_row = attn_gain, moe_gain
    layouts, routings = [], []
    for micro in (section, 1 - section):
        layouts.append(layout_tables(lax.dynamic_index_in_dim(lengths[:, 0], micro, 0, keepdims=False)))
        routings.append(
            routing_tables(
                lax.dynamic_index_in_dim(route_all, micro, 1, keepdims=False),
                lax.dynamic_index_in_dim(gate_all, micro, 1, keepdims=False),
                col,
            )
        )

    kept, forward_rows = [], []
    packed = packed0
    grad_all = None
    for step in range(3):
        which = step % 2
        flat = packed.reshape(PACK, D)
        part, n1, q, kv, mixed = run_attention(flat, weights, attn_row, layouts[which])
        resid, rows = run_attended(part.reshape(ROWS, TOK, D), packed, moe_row)
        part, xs, g, u = run_experts(rows.reshape(D, D), routings[which], mats)
        part = part.reshape(COLS, TOK, D)
        kept.append((flat, n1, q, kv, mixed, resid, xs, g, u))
        if step < 2:
            nexth, packed = run_mixed(part, resid, ends[1 - step])
        else:
            nexth, grad_all = run_last_mixed(part, resid, ends[0])
        forward_rows.append(nexth)

    entry = ends[0]
    backward_rows, pieces, moe_gains, attn_gains = [], [], [], []
    for step in range(3):
        which = (step + 1) % 2
        flat, n1, q, kv, mixed, resid, xs, g, u = kept[1 + step % 2]
        part, dy, dg, du, z = run_experts_back(grad_all.reshape(D, D), routings[which], g, u, mats)
        if step > 0:
            pieces.append((xs, dg, du, z, dy))
        if step == 2:
            expert_part = run_expert_weights(*zip(*pieces))
            expert_sum = lax.psum_scatter(expert_part, "row", scatter_dimension=0, tiled=True)
        dr, dgain, da = run_normed_back(part.reshape(COLS, TOK, D), resid, entry, moe_row)
        da = da.reshape(PACK, D)
        part, dp, again = run_attention_back(da, flat, weights, attn_row, layouts[which], q, kv)
        part = part.reshape(ROWS, TOK, D)
        if step > 0:
            moe_gains.append(dgain)
            attn_gains.append(again)
            pieces[-1] = pieces[-1] + (n1, dp, da, mixed)
        if step < 2:
            dhin, entry, grad_all = run_input_back(part, dr, ends[1 - step])
        else:
            dhin = run_last_back(part, dr)
        backward_rows.append(dhin)

    first, second = pieces[0][5:], pieces[1][5:]
    attn_part = call_local(
        attention_weights_kernel, [sds((D, 768), BF)], 10**9,
        *[item for pair in zip(first, second) for item in pair],
    )[0]
    gains = jnp.concatenate([attn_gains[0] + attn_gains[1], moe_gains[0] + moe_gains[1]], axis=0)
    attn_sum, gain_sum = run_weights_sum(attn_part.reshape(COLS, TOK, 768), gains)
    on_first = section == 0
    ends_out = jnp.stack(
        [jnp.where(on_first, backward_rows[m + 1], forward_rows[m + 1]) for m in range(2)], axis=0
    )[None, :, None]
    expert_sum = expert_sum[0].astype(F32)
    return (
        ends_out,
        attn_sum[None, :, 0:256],
        attn_sum[None, :, 256:384],
        attn_sum[None, :, 384:512],
        attn_sum[None, :, 512:768],
        gain_sum[0:1],
        gain_sum[1:2],
        expert_sum[0][None],
        expert_sum[1][None],
        jnp.swapaxes(expert_sum[2], 1, 2)[None],
    )


def solution(mesh):
    tokens = P("section", None, "col", "row", None)
    mats = P("section", "col", "row")
    gain = P("section", None)
    experts = P("section", "col", None, None)
    by_row = P("section", "col", "row", None)
    return jax.shard_map(
        per_device,
        mesh=mesh,
        in_specs=(tokens, mats, mats, mats, mats, gain, gain, experts, experts, experts, tokens, tokens, P(None, "col", None)),
        out_specs=(tokens, mats, mats, mats, mats, gain, gain, by_row, by_row, P("section", "col", None, "row")),
        check_vma=False,
    )
```

time: 1120 us -> 565 us (0.50)
  Pallas kernels: 0 us -> 498 us
  waiting for transfers between devices: 384 us -> 0.02 us
  blocking collectives: 351 us -> 0 us
  matrix products: 122 us -> 0.25 us
  starting transfers between devices: 90.2 us -> 0.04 us
  other arithmetic: 60.8 us -> 6.04 us
  local copies, waits for them, and re-layouts: 85.2 us -> 38.9 us
    pallas_call x0 -> x28, Pallas kernels: none -> 498 us  [the longest x14 396 us: call_remote(): pl.pallas_call(kernel, out_shape=outs, in_specs=[VM] * len(args), out_spe...]
    reduce_scatter x13 -> x1, waiting for transfers between devices: 196 us -> 0.01 us  [per_device(): lax.psum_scatter(expert_part, 'row', scatter_dimension=0, tiled=True)]
    all_to_all x11 -> x0, waiting for transfers between devices: 181 us -> none  [the longest x3 58.1 us: layer_forward(): lax.all_to_all(produced, 'col', split_axis=1, concat_axis=0, tiled=True)]
    psum x1 -> x0, blocking collectives: 165 us -> none  [sum_gains(): return lax.psum((grads_two[0], grads_two[1]), ('row', 'col'))]
    all_gather x10 -> x0, blocking collectives: 155 us -> none  [the longest x3 33 us: layer_forward(): packed = lax.all_gather(quarter_rows, 'row', axis=0, tiled=True)]
    dot_general x96 -> x2, matrix products: 122 us -> 0.25 us  [routing_tables(): jnp.einsum('est,tu->esu', chosen.astype(BF), before, preferred_element_ty...]
    all_to_all x11 -> x0, starting transfers between devices: 80.2 us -> none  [the longest x3 33.6 us: layer_backward(): lax.all_to_all(grad_back, 'col', split_axis=0, concat_axis=1, tiled=True)]
    all_to_all x1 -> x0, blocking collectives: 31.6 us -> none  [layer_forward(): lax.all_to_all(sending, 'col', split_axis=0, concat_axis=1, tiled=True)]
  transfers between devices with their start and end apart: 28 -> 1, of which waited for: 24 -> 0; matrix products, arithmetic and copies ran while one was open for 12% -> 0% of each run, Pallas kernels for 0% -> 14%
where the time goes in v1:
time: 565 us; the launch traced here: 559 us
  Pallas kernels  498 us (88%)
  local copies, waits for them, and re-layouts  38.9 us (7%)
  between operations  15.6 us (3%)
  other arithmetic  6.04 us (1%)
    pallas_call x14, Pallas kernels, call_remote(): pl.pallas_call(kernel, out_shape=outs, in_specs=[VM] * len(args), out_spe...  396 us
    pallas_call x6, Pallas kernels, call_experts(): pl.pallas_call(kernel, grid=(2,), out_shape=[shape for shape, _ in outs],...  73.3 us
    unnamed x130, local copies, waits for them, and re-layouts  28.6 us
    pallas_call x7, Pallas kernels, call_local(): pl.pallas_call(kernel, out_shape=outs, in_specs=[VM] * len(args), out_spe...  17.6 us
    pallas_call x1, Pallas kernels, run_expert_weights(): pl.pallas_call(expert_weights_kernel, grid=(2,), out_shape=out, in_specs=...  11.5 us
  transfers between devices with their start and end apart: 1, of which 0 were waited for; matrix products, arithmetic and copies ran while one was open for 0% of the time, Pallas kernels for 14%

profile of v1, /device:TPU:1, one launch (start us, length us, event | category | flops | bytes accessed | tf_op | source)
XLA Modules:
  0.0 558.8 jit_solution(72950348965868927)
XLA Ops:
  7.3 0.7 fusion.7
  8.5 0.7 convert_element_type.49
  9.6 0.8 copy.96
  11.7 23.1 %shard_map.204 = (bf16[16,64,768]{2,1,0:T(8,128)(2,1)S(1)}, f32[16,16,128]{2,1,0:T(8,128)S(1)}, bf16[4,64,1024]{2,1,0:T(8,128)(2,1)S(1)}) custom-call(bf16[64,768]{1,0:T(8,128)(2,1)S(1)} %pad_maximum_fusion.w_ref, f32[16,128]{1,0:T(8,128)S(1)} %pad_maximum_fusion.1.rg_ref, bf16[64,1024]{1,0:T(8,128)(2,1)S(1)} %get-tuple-element.200.x_ref.coming.entry), custom_call_target="tpu_custom_call" | custom-call | flops 1000000 | bytes 40000000 | tf_op jit(solution)/shard_map/pallas_call | solution.py:328
  34.9 1.2 copy-done.46
  40.2 0.9 reshape.393.gslot
  41.1 0.9 reshape.392.gslot
  42.1 1.4 copy-done.47
  43.5 2.7 shard_map.205
  46.1 28.1 %shard_map.206 = (f32[64,1024]{1,0:T(8,128)S(1)}, bf16[16,64,1024]{2,1,0:T(8,128)(2,1)S(1)}) custom-call(bf16[4,64,1024]{2,1,0:T(8,128)(2,1)S(1)} %bitcast.123, bf16[4,64,1024]{2,1,0:T(8,128)(2,1)S(1)} %get-tuple-element.77.packed, f32[1,1024]{1,0:T(1,128)S(1)} %copy-done.12), custom_call_target="tpu_custom_call" | custom-call | flops 1000000 | bytes 40000000 | tf_op jit(solution)/shard_map/pallas_call | solution.py:328
  74.2 1.3 copy-done.42
  75.5 1.2 and_convert_fusion
  76.7 12.0 %shard_map.207 = (bf16[1024,1024]{1,0:T(8,128)(2,1)}, bf16[2,384,1024]{2,1,0:T(8,128)(2,1)}, f32[2,384,512]{2,1,0:T(8,128)}, f32[2,384,512]{2,1,0:T(8,128)}) custom-call(bf16[1024,1024]{1,0:T(8,128)(2,1)} %bitcast.136, bf16[2,4,96,256]{3,2,1,0:T(8,128)(2,1)} %get-tuple-element.208.table, f32[2,384,1]{2,1,0:T(8,128)} %reshape.392.gslot, ...), custom_call_target="tpu_custom_call" | custom-call | flops 4000000000 | bytes 20000000 | tf_op jit(solution)/shard_map/pallas_call | solution.py:594
  88.7 1.6 copy-done.2
  90.2 31.1 %shard_map.208 = (bf16[64,1024]{1,0:T(8,128)(2,1)}, bf16[4,64,1024]{2,1,0:T(8,128)(2,1)S(1)}) custom-call(bf16[16,64,1024]{2,1,0:T(8,128)(2,1)S(1)} %bitcast.106, f32[64,1024]{1,0:T(8,128)S(1)} %get-tuple-element.83.resid, bf16[64,1024]{1,0:T(8,128)(2,1)S(1)} %get-tuple-element.199.coming), custom_call_target="tpu_custom_call" | custom-call | flops 1000000 | bytes 40000000 | tf_op jit(solution)/shard_map/pallas_call | solution.py:328
  121.4 2.0 shard_map.209
  123.4 0.6 copy-done.13
  124.1 27.7 %shard_map.210 = (f32[64,1024]{1,0:T(8,128)S(1)}, bf16[16,64,1024]{2,1,0:T(8,128)(2,1)S(1)}) custom-call(bf16[4,64,1024]{2,1,0:T(8,128)(2,1)S(1)} %bitcast.124, bf16[4,64,1024]{2,1,0:T(8,128)(2,1)S(1)} %get-tuple-element.84.packed, f32[1,1024]{1,0:T(1,128)S(1)} %copy-done.12), custom_call_target="tpu_custom_call" | custom-call | flops 1000000 | bytes 40000000 | tf_op jit(solution)/shard_map/pallas_call | solution.py:328
  151.8 1.3 copy-done.43
  153.1 11.5 %shard_map.211 = (bf16[1024,1024]{1,0:T(8,128)(2,1)}, bf16[2,384,1024]{2,1,0:T(8,128)(2,1)}, f32[2,384,512]{2,1,0:T(8,128)}, f32[2,384,512]{2,1,0:T(8,128)}) custom-call(bf16[1024,1024]{1,0:T(8,128)(2,1)} %bitcast.137, bf16[2,4,96,256]{3,2,1,0:T(8,128)(2,1)} %get-tuple-element.207.table, f32[2,384,1]{2,1,0:T(8,128)} %reshape.393.gslot, ...), custom_call_target="tpu_custom_call" | custom-call | flops 4000000000 | bytes 20000000 | tf_op jit(solution)/shard_map/pallas_call | solution.py:594
  164.7 1.6 copy-done.4
  166.3 31.3 %shard_map.212 = (bf16[64,1024]{1,0:T(8,128)(2,1)S(1)}, bf16[4,64,1024]{2,1,0:T(8,128)(2,1)S(1)}) custom-call(bf16[16,64,1024]{2,1,0:T(8,128)(2,1)S(1)} %bitcast.108, f32[64,1024]{1,0:T(8,128)S(1)} %get-tuple-element.88.resid, bf16[64,1024]{1,0:T(8,128)(2,1)S(1)} %get-tuple-element.200.x_ref.coming.entry), custom_call_target="tpu_custom_call" | custom-call | flops 1000000 | bytes 40000000 | tf_op jit(solution)/shard_map/pallas_call | solution.py:328
  197.6 0.6 copy-done.32
  198.2 2.0 shard_map.213
  200.3 0.6 copy-done.57
  200.9 27.3 %shard_map.214 = (f32[64,1024]{1,0:T(8,128)S(1)}, bf16[16,64,1024]{2,1,0:T(8,128)(2,1)S(1)}) custom-call(bf16[4,64,1024]{2,1,0:T(8,128)(2,1)S(1)} %bitcast.125, bf16[4,64,1024]{2,1,0:T(8,128)(2,1)S(1)} %get-tuple-element.89.packed, f32[1,1024]{1,0:T(1,128)S(1)} %copy-done.12), custom_call_target="tpu_custom_call" | custom-call | flops 1000000 | bytes 40000000 | tf_op jit(solution)/shard_map/pallas_call | solution.py:328
  228.2 1.3 copy-done.45
  229.6 11.7 %shard_map.215 = (bf16[1024,1024]{1,0:T(8,128)(2,1)}, bf16[2,384,1024]{2,1,0:T(8,128)(2,1)}, f32[2,384,512]{2,1,0:T(8,128)}, f32[2,384,512]{2,1,0:T(8,128)}) custom-call(bf16[1024,1024]{1,0:T(8,128)(2,1)} %bitcast.139, bf16[2,4,96,256]{3,2,1,0:T(8,128)(2,1)} %get-tuple-element.208.table, f32[2,384,1]{2,1,0:T(8,128)} %reshape.392.gslot, ...), custom_call_target="tpu_custom_call" | custom-call | flops 4000000000 | bytes 20000000 | tf_op jit(solution)/shard_map/pallas_call | solution.py:594
  241.3 1.6 copy-done.5
  242.8 36.3 %shard_map.216 = (bf16[64,1024]{1,0:T(8,128)(2,1)S(1)}, bf16[16,64,1024]{2,1,0:T(8,128)(2,1)S(1)}) custom-call(bf16[16,64,1024]{2,1,0:T(8,128)(2,1)S(1)} %bitcast.109, f32[64,1024]{1,0:T(8,128)S(1)} %get-tuple-element.93.resid, bf16[64,1024]{1,0:T(8,128)(2,1)S(1)} %get-tuple-element.200.x_ref.coming.entry), custom_call_target="tpu_custom_call" | custom-call | flops 1000000 | bytes 40000000 | tf_op jit(solution)/shard_map/pallas_call | solution.py:328
  279.1 0.6 copy-done.34
  279.8 1.3 copy-done.44
  281.1 12.6 %shard_map.217 = (bf16[1024,1024]{1,0:T(8,128)(2,1)}, bf16[2,384,1024]{2,1,0:T(8,128)(2,1)}, bf16[2,384,512]{2,1,0:T(8,128)(2,1)}, bf16[2,384,512]{2,1,0:T(8,128)(2,1)}, bf16[2,384,512]{2,1,0:T(8,128)(2,1)}) custom-call(bf16[1024,1024]{1,0:T(8,128)(2,1)} %bitcast.138, bf16[2,4,96,256]{3,2,1,0:T(8,128)(2,1)} %get-tuple-element.207.table, ...), custom_call_target="tpu_custom_call" | custom-call | flops 4000000000 | bytes 20000000 | tf_op jit(solution)/shard_map/pallas_call | solution.py:594
  293.7 1.6 copy-done.3
  295.3 27.4 %shard_map.218 = (f32[64,1024]{1,0:T(8,128)S(1)}, f32[1,1024]{1,0:T(1,128)}, bf16[4,64,1024]{2,1,0:T(8,128)(2,1)S(1)}) custom-call(bf16[16,64,1024]{2,1,0:T(8,128)(2,1)S(1)} %bitcast.107, f32[64,1024]{1,0:T(8,128)S(1)} %get-tuple-element.88.resid, bf16[64,1024]{1,0:T(8,128)(2,1)S(1)} %get-tuple-element.200.x_ref.coming.entry, f32[1,1024]{1,0:T(1,128)S(1)} %copy-done.12), custom_call_target="tpu_custom_call" | custom-call | flops 1000000 | bytes 40000000 | tf_op jit(solution)/shard_map/pallas_call | solution.py:328
  322.8 3.7 shard_map.219
  326.5 32.4 %shard_map.220 = (bf16[64,1024]{1,0:T(8,128)(2,1)}, bf16[64,1024]{1,0:T(8,128)(2,1)S(1)}, bf16[16,64,1024]{2,1,0:T(8,128)(2,1)S(1)}) custom-call(bf16[4,64,1024]{2,1,0:T(8,128)(2,1)S(1)} %bitcast.116, f32[64,1024]{1,0:T(8,128)S(1)} %get-tuple-element.102.dr, bf16[64,1024]{1,0:T(8,128)(2,1)S(1)} %get-tuple-element.199.coming), custom_call_target="tpu_custom_call" | custom-call | flops 1000000 | bytes 40000000 | tf_op jit(solution)/shard_map/pallas_call | solution.py:328
  358.9 1.3 copy-done.40
  360.2 12.8 %shard_map.221 = (bf16[1024,1024]{1,0:T(8,128)(2,1)}, bf16[2,384,1024]{2,1,0:T(8,128)(2,1)}, bf16[2,384,512]{2,1,0:T(8,128)(2,1)}, bf16[2,384,512]{2,1,0:T(8,128)(2,1)}, bf16[2,384,512]{2,1,0:T(8,128)(2,1)}) custom-call(bf16[1024,1024]{1,0:T(8,128)(2,1)} %bitcast.134, bf16[2,4,96,256]{3,2,1,0:T(8,128)(2,1)} %get-tuple-element.208.table, ...), custom_call_target="tpu_custom_call" | custom-call | flops 4000000000 | bytes 20000000 | tf_op jit(solution)/shard_map/pallas_call | solution.py:594
  373.0 1.6 copy-done.1
  374.6 27.1 %shard_map.222 = (f32[64,1024]{1,0:T(8,128)S(1)}, f32[1,1024]{1,0:T(1,128)S(1)}, bf16[4,64,1024]{2,1,0:T(8,128)(2,1)S(1)}) custom-call(bf16[16,64,1024]{2,1,0:T(8,128)(2,1)S(1)} %bitcast.105, f32[64,1024]{1,0:T(8,128)S(1)} %get-tuple-element.93.resid, bf16[64,1024]{1,0:T(8,128)(2,1)S(1)} %get-tuple-element.107.entry, f32[1,1024]{1,0:T(1,128)S(1)} %copy-done.12), custom_call_target="tpu_custom_call" | custom-call | flops 1000000 | bytes 40000000 | tf_op jit(solution)/shard_map/pallas_call | solution.py:328
  401.7 3.1 shard_map.223
  404.8 0.8 copy-done.6
  405.6 31.1 %shard_map.224 = (bf16[64,1024]{1,0:T(8,128)(2,1)S(1)}, bf16[64,1024]{1,0:T(8,128)(2,1)S(1)}, bf16[16,64,1024]{2,1,0:T(8,128)(2,1)S(1)}) custom-call(bf16[4,64,1024]{2,1,0:T(8,128)(2,1)S(1)} %bitcast.114, f32[64,1024]{1,0:T(8,128)S(1)} %get-tuple-element.112.dr, bf16[64,1024]{1,0:T(8,128)(2,1)S(1)} %get-tuple-element.200.x_ref.coming.entry), custom_call_target="tpu_custom_call" | custom-call | flops 1000000 | bytes 40000000 | tf_op jit(solution)/shard_map/pallas_call | solution.py:328
  436.8 0.6 copy-done.17
  437.4 0.7 copy-done.36
  438.1 1.3 copy-done.41
  439.4 12.7 %shard_map.225 = (bf16[1024,1024]{1,0:T(8,128)(2,1)}, bf16[2,384,1024]{2,1,0:T(8,128)(2,1)}, bf16[2,384,512]{2,1,0:T(8,128)(2,1)}, bf16[2,384,512]{2,1,0:T(8,128)(2,1)}, bf16[2,384,512]{2,1,0:T(8,128)(2,1)}) custom-call(bf16[1024,1024]{1,0:T(8,128)(2,1)} %bitcast.135, bf16[2,4,96,256]{3,2,1,0:T(8,128)(2,1)} %get-tuple-element.207.table, ...), custom_call_target="tpu_custom_call" | custom-call | flops 4000000000 | bytes 20000000 | tf_op jit(solution)/shard_map/pallas_call | solution.py:594
  452.1 11.5 %shard_map.231 = bf16[4,3,2,256,512]{4,3,2,1,0:T(8,128)(2,1)} custom-call(bf16[2,384,1024]{2,1,0:T(8,128)(2,1)} %get-tuple-element.134.xa, bf16[2,384,1024]{2,1,0:T(8,128)(2,1)} %get-tuple-element.135.xb, bf16[2,384,512]{2,1,0:T(8,128)(2,1)} %get-tuple-element.136.ga, bf16[2,384,512]{2,1,0:T(8,128)(2,1)} %get-tuple-element.137.gb, ...), custom_call_target="tpu_custom_call" | custom-call | flops 5000000000 | bytes 20000000 | tf_op jit(solution)/shard_map/pallas_call | solution.py:657
  463.7 1.5 copy-done
  465.2 31.9 %shard_map.226 = (f32[64,1024]{1,0:T(8,128)S(1)}, f32[1,1024]{1,0:T(1,128)S(1)}, bf16[4,64,1024]{2,1,0:T(8,128)(2,1)S(1)}) custom-call(bf16[16,64,1024]{2,1,0:T(8,128)(2,1)S(1)} %bitcast.104, f32[64,1024]{1,0:T(8,128)S(1)} %get-tuple-element.88.resid, bf16[64,1024]{1,0:T(8,128)(2,1)S(1)} %copy-done.18, f32[1,1024]{1,0:T(1,128)S(1)} %copy-done.12), custom_call_target="tpu_custom_call" | custom-call | flops 1000000 | bytes 40000000 | tf_op jit(solution)/shard_map/pallas_call | solution.py:328
  497.1 0.9 copy-done.54
  498.0 0.9 copy-done.56
  498.9 3.1 shard_map.227
  502.0 15.1 %shard_map.228 = bf16[64,1024]{1,0:T(8,128)(2,1)S(1)} custom-call(bf16[4,64,1024]{2,1,0:T(8,128)(2,1)S(1)} %bitcast.115, f32[64,1024]{1,0:T(8,128)S(1)} %get-tuple-element.120.dr), custom_call_target="tpu_custom_call" | custom-call | flops 1000000 | bytes 40000000 | tf_op jit(solution)/shard_map/pallas_call | solution.py:328
  517.2 1.1 shard_map.229
  518.3 25.7 %shard_map.230 = (f32[64,768]{1,0:T(8,128)S(1)}, f32[2,1024]{1,0:T(2,128)S(1)}) custom-call(bf16[16,64,768]{2,1,0:T(8,128)(2,1)S(1)} %bitcast.103, f32[2,1024]{1,0:T(2,128)S(1)} %pad_maximum_fusion.2.gains), custom_call_target="tpu_custom_call" | custom-call | flops 1000000 | bytes 40000000 | tf_op jit(solution)/shard_map/pallas_call | solution.py:328
  544.1 0.7 maximum_bitcast_fusion
  544.8 0.6 fusion.10
  545.4 0.6 slice_bitcast_fusion.7
  546.1 0.7 slice_bitcast_fusion.5
  546.7 1.8 convert_element_type.59
  548.6 1.6 slice_bitcast_fusion
  550.2 1.3 copy.128
  (160 shorter events, 6.3 us)
Async XLA Ops:
  7.2 4.4 copy-start.59
  7.2 4.5 copy-start.60
  7.2 4.5 copy-start.62
  7.2 4.5 copy-start.63
  7.2 4.5 copy-start.61
  7.2 539.5 %reduce-scatter.2.cloned.1.call-start = ((), (), s32[]{:S(2)}) async-start(), calls=%async_computation.1 | async-start | bytes 7864320 | tf_op jit(solution)/shard_map/reduce_scatter | solution.py:753
  10.9 311.8 %copy-start.19 = (f32[256,128]{1,0:T(8,128)}, f32[256,128]{1,0:T(8,128)S(1)}, u32[]{:S(2)}) copy-start(f32[256,128]{1,0:T(8,128)S(1)} %copy.106.sine) | copy-start | bytes 393220
  11.1 31.0 %copy-start.26 = (s32[256,1]{1,0:T(8,128)}, s32[256,1]{1,0:T(8,128)S(1)}, u32[]{:S(2)}) copy-start(s32[256,1]{1,0:T(8,128)S(1)} %copy.99.seg) | copy-start | bytes 3076
  11.2 311.5 %copy-start.21 = (s32[256,1]{1,0:T(8,128)}, s32[256,1]{1,0:T(8,128)S(1)}, u32[]{:S(2)}) copy-start(s32[256,1]{1,0:T(8,128)S(1)} %copy.107.seg) | copy-start | bytes 3076
  11.4 110.0 %copy-start.23 = (f32[256,128]{1,0:T(8,128)}, f32[256,128]{1,0:T(8,128)S(1)}, u32[]{:S(2)}) copy-start(f32[256,128]{1,0:T(8,128)S(1)} %copy.105.cosine) | copy-start | bytes 393220
  11.5 30.6 %copy-start.28 = (f32[256,128]{1,0:T(8,128)}, f32[256,128]{1,0:T(8,128)S(1)}, u32[]{:S(2)}) copy-start(f32[256,128]{1,0:T(8,128)S(1)} %copy.97.cosine) | copy-start | bytes 393220
  11.6 30.4 %copy-start.30 = (f32[256,128]{1,0:T(8,128)}, f32[256,128]{1,0:T(8,128)S(1)}, u32[]{:S(2)}) copy-start(f32[256,128]{1,0:T(8,128)S(1)} %copy.98.sine) | copy-start | bytes 393220
  34.9 1.2 copy-start.46
  37.0 5.0 copy-start.50
  41.1 5.0 copy-start.12
  42.1 1.4 copy-start.47
  74.2 1.3 copy-start.42
  76.7 44.7 %copy-start.48 = (bf16[16,64,768]{2,1,0:T(8,128)(2,1)S(1)}, bf16[16,64,768]{2,1,0:T(8,128)(2,1)}, u32[]{:S(2)}) copy-start(bf16[16,64,768]{2,1,0:T(8,128)(2,1)} %copy-done.46) | copy-start | bytes 4718596
  88.6 1.6 copy-start.2
  121.3 201.4 %copy-start.8 = (bf16[4,64,1024]{2,1,0:T(8,128)(2,1)}, bf16[4,64,1024]{2,1,0:T(8,128)(2,1)S(1)}, u32[]{:S(2)}) copy-start(bf16[4,64,1024]{2,1,0:T(8,128)(2,1)S(1)} %get-tuple-element.84.packed) | copy-start | bytes 1572868
  123.4 0.7 copy-start.13
  124.1 198.7 %copy-start.53 = (bf16[256,256]{1,0:T(8,128)(2,1)}, bf16[256,256]{1,0:T(8,128)(2,1)S(1)}, u32[]{:S(2)}) copy-start(bf16[256,256]{1,0:T(8,128)(2,1)S(1)} %get-tuple-element.99.q_ref) | copy-start | bytes 393220
  124.1 198.7 %copy-start.55 = (bf16[256,256]{1,0:T(8,128)(2,1)}, bf16[256,256]{1,0:T(8,128)(2,1)S(1)}, u32[]{:S(2)}) copy-start(bf16[256,256]{1,0:T(8,128)(2,1)S(1)} %get-tuple-element.100.kv_ref) | copy-start | bytes 393220
  151.8 1.3 copy-start.43
  153.1 45.1 %copy-start.27 = (s32[256,1]{1,0:T(8,128)S(1)}, s32[256,1]{1,0:T(8,128)}, u32[]{:S(2)}) copy-start(s32[256,1]{1,0:T(8,128)} %copy-done.26) | copy-start | bytes 3076
  153.1 45.1 %copy-start.29 = (f32[256,128]{1,0:T(8,128)S(1)}, f32[256,128]{1,0:T(8,128)}, u32[]{:S(2)}) copy-start(f32[256,128]{1,0:T(8,128)} %copy-done.28) | copy-start | bytes 393220
  153.1 45.1 %copy-start.31 = (f32[256,128]{1,0:T(8,128)S(1)}, f32[256,128]{1,0:T(8,128)}, u32[]{:S(2)}) copy-start(f32[256,128]{1,0:T(8,128)} %copy-done.30) | copy-start | bytes 393220
  164.7 1.6 copy-start.4
  197.6 0.7 copy-start.32
  200.3 0.6 copy-start.57
  200.9 40.3 %copy-start.15 = (bf16[256,256]{1,0:T(8,128)(2,1)}, bf16[256,256]{1,0:T(8,128)(2,1)S(1)}, u32[]{:S(2)}) copy-start(bf16[256,256]{1,0:T(8,128)(2,1)S(1)} %get-tuple-element.126.oa) | copy-start | bytes 393220
  228.2 1.3 copy-start.45
  241.3 1.6 copy-start.5
  279.1 0.6 copy-start.34
  279.8 1.3 copy-start.44
  281.1 41.7 %copy-start.24 = (f32[256,128]{1,0:T(8,128)S(1)}, f32[256,128]{1,0:T(8,128)}, u32[]{:S(2)}) copy-start(f32[256,128]{1,0:T(8,128)} %copy-done.23) | copy-start | bytes 393220
  293.7 1.6 copy-start.3
  358.9 1.3 copy-start.40
  360.2 41.5 %copy-start.58 = (bf16[256,256]{1,0:T(8,128)(2,1)S(1)}, bf16[256,256]{1,0:T(8,128)(2,1)}, u32[]{:S(2)}) copy-start(bf16[256,256]{1,0:T(8,128)(2,1)} %copy-done.57) | copy-start | bytes 393220
  373.0 28.7 %copy-start.51 = (f32[1,1024]{1,0:T(1,128)S(1)}, f32[1,1024]{1,0:T(1,128)}, u32[]{:S(2)}) copy-start(f32[1,1024]{1,0:T(1,128)} %gain.23) | copy-start | bytes 12292
  373.0 1.6 copy-start.1
  401.7 35.1 %copy-start.38 = (f32[1,1024]{1,0:T(1,128)}, f32[1,1024]{1,0:T(1,128)S(1)}, u32[]{:S(2)}) copy-start(f32[1,1024]{1,0:T(1,128)S(1)} %get-tuple-element.130) | copy-start | bytes 12292
  404.8 0.8 copy-start.6
  405.6 31.2 %copy-start.10 = (bf16[256,512]{1,0:T(8,128)(2,1)}, bf16[256,512]{1,0:T(8,128)(2,1)S(1)}, u32[]{:S(2)}) copy-start(bf16[256,512]{1,0:T(8,128)(2,1)S(1)} %get-tuple-element.124.pa) | copy-start | bytes 786436
  437.4 0.7 copy-start.36
  438.1 1.3 copy-start.41
  463.6 1.6 copy-start
  463.6 1.6 copy-start.18
  463.6 33.4 %copy-start.39 = (f32[1,1024]{1,0:T(1,128)S(1)}, f32[1,1024]{1,0:T(1,128)}, u32[]{:S(2)}) copy-start(f32[1,1024]{1,0:T(1,128)} %copy-done.38) | copy-start | bytes 12292
  463.6 33.4 %copy-start.9 = (bf16[4,64,1024]{2,1,0:T(8,128)(2,1)S(1)}, bf16[4,64,1024]{2,1,0:T(8,128)(2,1)}, u32[]{:S(2)}) copy-start(bf16[4,64,1024]{2,1,0:T(8,128)(2,1)} %copy-done.8) | copy-start | bytes 1572868
  463.6 33.4 %copy-start.20 = (f32[256,128]{1,0:T(8,128)S(1)}, f32[256,128]{1,0:T(8,128)}, u32[]{:S(2)}) copy-start(f32[256,128]{1,0:T(8,128)} %copy-done.19) | copy-start | bytes 393220
  463.6 33.4 %copy-start.22 = (s32[256,1]{1,0:T(8,128)S(1)}, s32[256,1]{1,0:T(8,128)}, u32[]{:S(2)}) copy-start(s32[256,1]{1,0:T(8,128)} %copy-done.21) | copy-start | bytes 3076
  463.7 33.4 %copy-start.25 = (f32[256,128]{1,0:T(8,128)S(1)}, f32[256,128]{1,0:T(8,128)}, u32[]{:S(2)}) copy-start(f32[256,128]{1,0:T(8,128)} %copy-done.23) | copy-start | bytes 393220
  463.7 33.4 %copy-start.49 = (bf16[16,64,768]{2,1,0:T(8,128)(2,1)S(1)}, bf16[16,64,768]{2,1,0:T(8,128)(2,1)}, u32[]{:S(2)}) copy-start(bf16[16,64,768]{2,1,0:T(8,128)(2,1)} %copy-done.46) | copy-start | bytes 4718596
  463.7 33.4 %copy-start.52 = (f32[1,1024]{1,0:T(1,128)S(1)}, f32[1,1024]{1,0:T(1,128)}, u32[]{:S(2)}) copy-start(f32[1,1024]{1,0:T(1,128)} %gain.23) | copy-start | bytes 12292
  497.1 0.9 copy-start.54
  498.0 0.9 copy-start.56
  498.9 18.2 %copy-start.7 = (bf16[4,64,1024]{2,1,0:T(8,128)(2,1)S(1)}, bf16[4,64,1024]{2,1,0:T(8,128)(2,1)}, u32[]{:S(2)}) copy-start(bf16[4,64,1024]{2,1,0:T(8,128)(2,1)} %copy-done.6) | copy-start | bytes 1572868
  498.9 18.2 %copy-start.11 = (bf16[256,512]{1,0:T(8,128)(2,1)S(1)}, bf16[256,512]{1,0:T(8,128)(2,1)}, u32[]{:S(2)}) copy-start(bf16[256,512]{1,0:T(8,128)(2,1)} %copy-done.10) | copy-start | bytes 786436
  498.9 18.2 %copy-start.14 = (bf16[256,256]{1,0:T(8,128)(2,1)S(1)}, bf16[256,256]{1,0:T(8,128)(2,1)}, u32[]{:S(2)}) copy-start(bf16[256,256]{1,0:T(8,128)(2,1)} %copy-done.13) | copy-start | bytes 393220
  498.9 18.2 %copy-start.16 = (bf16[256,256]{1,0:T(8,128)(2,1)S(1)}, bf16[256,256]{1,0:T(8,128)(2,1)}, u32[]{:S(2)}) copy-start(bf16[256,256]{1,0:T(8,128)(2,1)} %copy-done.15) | copy-start | bytes 393220
  517.2 26.9 %copy-start.33 = (bf16[64,1024]{1,0:T(8,128)(2,1)S(1)}, bf16[64,1024]{1,0:T(8,128)(2,1)}, u32[]{:S(2)}) copy-start(bf16[64,1024]{1,0:T(8,128)(2,1)} %copy-done.32) | copy-start | bytes 393220
  517.2 26.9 %copy-start.37 = (bf16[64,1024]{1,0:T(8,128)(2,1)S(1)}, bf16[64,1024]{1,0:T(8,128)(2,1)}, u32[]{:S(2)}) copy-start(bf16[64,1024]{1,0:T(8,128)(2,1)} %copy-done.36) | copy-start | bytes 393220
  517.2 26.9 %copy-start.35 = (bf16[64,1024]{1,0:T(8,128)(2,1)S(1)}, bf16[64,1024]{1,0:T(8,128)(2,1)}, u32[]{:S(2)}) copy-start(bf16[64,1024]{1,0:T(8,128)(2,1)} %copy-done.34) | copy-start | bytes 393220
  (1 other events, 0.6 us)
Sparse Core Ops, SparseCore 0:
  463.7 72.4 reduce-scatter.1

commit v2 on v1

v2 whole, which is shorter than its diff:
```python
import functools

import jax
import jax.numpy as jnp
from jax import lax
from jax.experimental import pallas as pl
from jax.experimental.pallas import tpu as pltpu
from jax.sharding import PartitionSpec as P

D = 1024
FF = 512
HEAD = 64
TOK = 64
ROWS = 4
COLS = 16
CHIPS = 8
CAP = 24
PACK = 256
SLOTS = COLS * CAP
QUADS = 4

SCORE_MUL = 0.015625
RESID_MUL = 0.22
NORM_EPS = 1e-06
ROPE_THETA = 10000.0
MESH = pl.DeviceIdType.MESH
BF = jnp.bfloat16
F32 = jnp.float32
VM = pl.BlockSpec(memory_space=pltpu.VMEM)
DMA = pltpu.SemaphoreType.DMA


def dot(a, b):
    return jnp.dot(a, b, preferred_element_type=F32)


def dot_rows(a, b):
    return lax.dot_general(a, b, (((0,), (0,)), ((), ())), preferred_element_type=F32)


def dot_cols(a, b):
    return lax.dot_general(a, b, (((1,), (1,)), ((), ())), preferred_element_type=F32)


class Place:
    def __init__(self):
        self.section = lax.axis_index("section")
        self.row = lax.axis_index("row")
        self.col = lax.axis_index("col")
        self.high = self.col // 8
        self.deep = lax.rem(self.col // 2, 4)
        self.core = lax.rem(self.col, 2)

    def row_at(self, step):
        return lax.rem(self.row + step + ROWS, ROWS)

    def row_peer(self, step):
        return (self.section, self.row_at(step), self.col)

    def at(self, high, deep, core=0):
        high = lax.rem(self.high + high, 2)
        deep = lax.rem(self.deep + deep + 4, 4)
        return high * 8 + deep * 2 + lax.rem(self.core + core, 2)

    def peer(self, high, deep, core=0):
        return (self.section, self.row, self.at(high, deep, core))

    def across(self):
        return (1 - self.section, self.row, self.col)


def greet(partners):
    barrier = pltpu.get_barrier_semaphore()
    for partner in partners:
        pl.semaphore_signal(barrier, inc=1, device_id=partner, device_id_type=MESH)
    pl.semaphore_wait(barrier, len(partners))


def remote(src, dst, sems, index, device):
    return pltpu.make_async_remote_copy(
        src_ref=src, dst_ref=dst, send_sem=sems[0].at[index], recv_sem=sems[1].at[index],
        device_id=device, device_id_type=MESH,
    )


def send(src, dst, sems, index, device):
    copy = remote(src, dst, sems, index, device)
    copy.start()
    return copy


def finish(copies):
    for copy in copies:
        copy.wait_send()


def row_partners(me):
    return [me.row_peer(step) for step in (1, 2, 3)]


def col_partners(me):
    return [me.peer(0, 1), me.peer(0, 2), me.peer(0, 3), me.peer(1, 0), me.peer(0, 0, 1)]


def all_chip_partners(me):
    return [me.peer(high, deep) for high in range(2) for deep in range(4) if high or deep]


ROW_SEMS = [DMA((3,)), DMA((3,))]
COL_SEMS = [DMA((7,)), DMA((7,)), DMA((8,)), DMA((8,))]
NEAR = ((1, 0), (3, 1), (2, 2))


def weave(*chains):
    chains = list(chains)
    while chains:
        chains = [chain for chain in chains if next(chain, "end") != "end"]


def gather_row(me, out, sems):
    copies = []
    for step in (2, 1, 3):
        copies.append(send(out.at[me.row], out.at[me.row], sems, step - 1, me.row_peer(step)))
    yield
    for step in (1, 3, 2):
        origin = me.row_at(-step)
        remote(out.at[origin], out.at[origin], sems, step - 1, me.row_peer(step)).wait_recv()
    finish(copies)


def gather_col(me, out, sems):
    main, side = sems[0:2], sems[2:4]
    own = out.at[me.col]
    copies = [send(own, own, main, 3, me.peer(1, 0))]
    for deep, index in NEAR:
        copies.append(send(own, own, main, index, me.peer(0, deep)))
    copies.append(send(own, own, side, 0, me.peer(0, 0, 1)))
    yield
    far = out.at[me.at(1, 0)]
    remote(far, far, main, 3, me.peer(1, 0)).wait_recv()
    for deep, index in NEAR:
        copies.append(send(far, far, main, 4 + index, me.peer(0, deep)))
    copies.append(send(far, far, side, 4, me.peer(0, 0, 1)))
    yield
    for high in range(2):
        for deep, index in NEAR:
            block = out.at[me.at(high, -deep)]
            remote(block, block, main, 4 * high + index, me.peer(0, deep)).wait_recv()
            copies.append(send(block, block, side, 4 * high + 1 + index, me.peer(0, 0, 1)))
    yield
    for high in range(2):
        for deep, index in ((0, -1),) + NEAR:
            block = out.at[me.at(high, -deep, 1)]
            remote(block, block, side, 4 * high + 1 + index, me.peer(0, 0, 1)).wait_recv()
    finish(copies)


def sum_row(me, part, landing, sems, done):
    copies = []
    for step in (2, 1, 3):
        copies.append(send(part.at[me.row_at(step)], landing.at[step - 1], sems, step - 1, me.row_peer(step)))
    yield
    total = part[me.row].astype(F32)
    for copy, step in zip(copies[1:] + copies[:1], (1, 3, 2)):
        copy.wait_recv()
        total = total + landing[step - 1].astype(F32)
    yield from done(total)
    finish(copies)


def sum_col(me, part, halves, outgoing, landing, sems, done):
    main, side = sems[0:2], sems[2:4]
    order = [(high, deep) for high in (1, 0) for deep in (2, 1, 3, 0)]
    first = {}
    for high, deep in order:
        index = 4 * high + deep
        first[index] = send(part.at[me.at(high, deep, 1)], halves.at[index], side, index, me.peer(0, 0, 1))
    yield
    away = {}
    for high in (1, 0):
        for deep in (2, 1, 3):
            index, slot = 4 * high + deep, 3 * high + deep - 1
            first[index].wait_recv()
            outgoing[slot] = (part[me.at(high, deep)].astype(F32) + halves[index].astype(F32)).astype(BF)
            away[slot] = send(outgoing.at[slot], landing.at[slot], main, slot, me.peer(0, deep))
    yield
    first[4].wait_recv()
    total = part[me.at(1, 0)].astype(F32) + halves[4].astype(F32)
    for slot in (3, 5, 4):
        away[slot].wait_recv()
        total = total + landing[slot].astype(F32)
    outgoing[6] = total.astype(BF)
    away[6] = send(outgoing.at[6], landing.at[6], main, 6, me.peer(1, 0))
    yield
    first[0].wait_recv()
    total = part[me.col].astype(F32) + halves[0].astype(F32)
    for slot in (0, 2, 1, 6):
        away[slot].wait_recv()
        total = total + landing[slot].astype(F32)
    yield from done(total)
    finish(list(first.values()) + list(away.values()))


def sum_col_scratch(width):
    return [
        pltpu.VMEM((8, TOK, width), BF),
        pltpu.VMEM((7, TOK, width), BF),
        pltpu.VMEM((7, TOK, width), BF),
    ]


def store(ref):
    def done(total):
        ref[...] = total
        yield

    return done


def after_attention(me, h_ref, gain, other, resid, out, sems):
    def done(total):
        value = h_ref[me.row].astype(F32) + RESID_MUL * total
        resid[...] = value
        scale = lax.rsqrt(jnp.mean(value * value, axis=1, keepdims=True) + NORM_EPS)
        normed = (value * scale * gain[...]).astype(BF)
        if other is not None:
            normed = jnp.where(me.section == 0, normed, other[...])
        out[me.col] = normed
        yield from gather_col(me, out, sems)

    return done


def after_experts(me, resid, coming, nexth, out, arrived, over_sems, sems):
    def done(total):
        nexth[...] = (resid[...] + RESID_MUL * total).astype(BF)
        if out is not None:
            over = send(nexth, arrived, over_sems, 0, me.across())
            yield
            over.wait_recv()
            out[me.row] = jnp.where(me.section == 0, coming[...], arrived[...])
            yield from gather_row(me, out, sems)
            over.wait_send()
        else:
            yield

    return done


def after_experts_back(me, resid, entry, gain, dr, dgain, out, sems):
    def done(total):
        value = resid[...]
        scale = lax.rsqrt(jnp.mean(value * value, axis=1, keepdims=True) + NORM_EPS)
        weighted = total * gain[...]
        inner = jnp.mean(weighted * value, axis=1, keepdims=True)
        grad = entry[...].astype(F32) + scale * weighted - value * (scale * scale * scale) * inner
        out[me.row] = (RESID_MUL * grad).astype(BF)
        gather = gather_row(me, out, sems)
        next(gather)
        dr[...] = grad
        dgain[...] = jnp.sum(total * value * scale, axis=0, keepdims=True)
        yield
        yield from gather

    return done


def after_attention_back(me, dr, coming, dhin, entry, out, arrived, over_sems, sems):
    def done(total):
        dhin[...] = (total + dr[...]).astype(BF)
        if out is not None:
            over = send(dhin, arrived, over_sems, 0, me.across())
            yield
            over.wait_recv()
            chosen = jnp.where(me.section == 0, arrived[...], coming[...])
            entry[...] = chosen
            out[me.col] = chosen
            yield from gather_col(me, out, sems)
            over.wait_send()
        else:
            yield

    return done


def start_kernel(w_ref, rg_ref, x_ref, w_out, rg_out, x_out, *sems):
    me = Place()
    greet(row_partners(me) + col_partners(me))
    w_out[me.col] = w_ref[...]
    rg_out[me.col] = rg_ref[...]
    x_out[me.row] = x_ref[...]
    weave(
        gather_col(me, w_out, sems[6:10]),
        gather_row(me, x_out, sems[0:2]),
        gather_col(me, rg_out, sems[2:6]),
    )


def first_attended_kernel(part, packed, gain, other, resid, out, landing, *sems):
    me = Place()
    greet(row_partners(me) + col_partners(me))
    done = after_attention(me, packed, gain, other, resid, out, sems[2:6])
    weave(sum_row(me, part, landing, sems[0:2], done))


def attended_kernel(part, packed, gain, resid, out, landing, *sems):
    first_attended_kernel(part, packed, gain, None, resid, out, landing, *sems)


def mixed_kernel(part, resid, coming, nexth, out, arrived, halves, outgoing, landing, *sems):
    me = Place()
    greet(row_partners(me) + col_partners(me) + [me.across()])
    done = after_experts(me, resid, coming, nexth, out, arrived, sems[6:8], sems[0:2])
    weave(sum_col(me, part, halves, outgoing, landing, sems[2:6], done))


def turn_one_kernel(
    part_f, packed, part_b, resid_b, entry, gain, resid, out, dr, dgain, da,
    landing_row, halves, outgoing, landing, *sems,
):
    me = Place()
    greet(row_partners(me) + col_partners(me))
    done_f = after_attention(me, packed, gain, None, resid, out, sems[2:6])
    done_b = after_experts_back(me, resid_b, entry, gain, dr, dgain, da, sems[6:8])
    weave(
        sum_row(me, part_f, landing_row, sems[0:2], done_f),
        sum_col(me, part_b, halves, outgoing, landing, sems[8:12], done_b),
    )


def turn_two_kernel(
    part_f, resid, part_b, dr, coming, nexth, dhin, entry, out,
    arrived, landing_row, halves, outgoing, landing, *sems,
):
    me = Place()
    greet(row_partners(me) + col_partners(me) + [me.across()])
    done_f = after_experts(me, resid, None, nexth, None, None, None, None)
    done_b = after_attention_back(me, dr, coming, dhin, entry, out, arrived, sems[12:14], sems[2:6])
    weave(
        sum_row(me, part_b, landing_row, sems[0:2], done_b),
        sum_col(me, part_f, halves, outgoing, landing, sems[8:12], done_f),
    )


def normed_back_kernel(part, resid, entry, gain, dr, dgain, out, halves, outgoing, landing, *sems):
    me = Place()
    greet(row_partners(me) + col_partners(me))
    done = after_experts_back(me, resid, entry, gain, dr, dgain, out, sems[0:2])
    weave(sum_col(me, part, halves, outgoing, landing, sems[2:6], done))


def input_back_kernel(part, dr, coming, dhin, entry, out, arrived, landing, *sems):
    me = Place()
    greet(row_partners(me) + col_partners(me) + [me.across()])
    done = after_attention_back(me, dr, coming, dhin, entry, out, arrived, sems[6:8], sems[2:6])
    weave(sum_row(me, part, landing, sems[0:2], done))


def sum_gains(me, gains, out, one, two, three, sems):
    near = send(gains, one, sems, 0, me.peer(0, 0, 1))
    yield
    near.wait_recv()
    two[0] = gains[...] + one[...]
    chips = []
    for high in range(2):
        for deep in range(4):
            if high or deep:
                index = high * 4 + deep
                chips.append(send(two.at[0], two.at[index], sems, index, me.peer(high, deep)))
    yield
    for copy in chips:
        copy.wait_recv()
    three[0] = jnp.sum(two[...], axis=0)
    rows = []
    for step in (1, 2, 3):
        rows.append(send(three.at[0], three.at[step], sems, 7 + step, me.row_peer(step)))
    yield
    for copy in rows:
        copy.wait_recv()
    out[...] = jnp.sum(three[...], axis=0)
    finish([near] + chips + rows)


def last_kernel(
    part_x, dr, part, gains, dhin, out, gains_out, landing_row, halves, outgoing, landing, one, two, three, *sems
):
    me = Place()
    greet(row_partners(me) + all_chip_partners(me) + [me.peer(0, 0, 1)])
    done = after_attention_back(me, dr, None, dhin, None, None, None, None, None)
    weave(
        sum_col(me, part, halves, outgoing, landing, sems[2:6], store(out)),
        sum_row(me, part_x, landing_row, sems[0:2], done),
        sum_gains(me, gains, gains_out, one, two, three, sems[6:8]),
    )


def call_remote(kernel, ident, outs, scratch, *args):
    return pl.pallas_call(
        kernel,
        out_shape=outs,
        in_specs=[VM] * len(args),
        out_specs=[VM] * len(outs),
        scratch_shapes=scratch,
        compiler_params=pltpu.CompilerParams(
            collective_id=ident, has_side_effects=True, vmem_limit_bytes=20 * 2**20
        ),
        cost_estimate=pl.CostEstimate(flops=10**6, bytes_accessed=40 * 10**6, transcendentals=0),
    )(*args)


def sds(shape, kind):
    return jax.ShapeDtypeStruct(shape, kind)


ACROSS = [DMA((1,)), DMA((1,))]
LAND_ROW = [pltpu.VMEM((3, TOK, D), BF)]
ARRIVED = [pltpu.VMEM((TOK, D), BF)]
TOKEN_ROWS = sds((TOK, D), BF)
TOKEN_WIDE = sds((TOK, D), F32)
ROW_BLOCKS = sds((ROWS, TOK, D), BF)
COL_BLOCKS = sds((COLS, TOK, D), BF)
GAIN = sds((1, D), F32)


def run_start(w, rg, x):
    return call_remote(
        start_kernel, 0, [sds((COLS,) + w.shape, BF), sds((COLS,) + rg.shape, F32), ROW_BLOCKS],
        ROW_SEMS + COL_SEMS + COL_SEMS, w, rg, x,
    )


def run_first_attended(part, packed, gain, other):
    return call_remote(
        first_attended_kernel, 1, [TOKEN_WIDE, COL_BLOCKS], LAND_ROW + ROW_SEMS + COL_SEMS,
        part, packed, gain, other,
    )


def run_attended(part, packed, gain):
    return call_remote(
        attended_kernel, 2, [TOKEN_WIDE, COL_BLOCKS], LAND_ROW + ROW_SEMS + COL_SEMS, part, packed, gain
    )


def run_mixed(part, resid, coming):
    return call_remote(
        mixed_kernel, 3, [TOKEN_ROWS, ROW_BLOCKS],
        ARRIVED + sum_col_scratch(D) + ROW_SEMS + COL_SEMS + ACROSS, part, resid, coming,
    )


def run_turn_one(part_f, packed, part_b, resid_b, entry, gain):
    return call_remote(
        turn_one_kernel, 4, [TOKEN_WIDE, COL_BLOCKS, TOKEN_WIDE, GAIN, ROW_BLOCKS],
        LAND_ROW + sum_col_scratch(D) + ROW_SEMS + COL_SEMS + ROW_SEMS + COL_SEMS,
        part_f, packed, part_b, resid_b, entry, gain,
    )


def run_turn_two(part_f, resid, part_b, dr, coming):
    return call_remote(
        turn_two_kernel, 5, [TOKEN_ROWS, TOKEN_ROWS, TOKEN_ROWS, COL_BLOCKS],
        ARRIVED + LAND_ROW + sum_col_scratch(D) + ROW_SEMS + COL_SEMS + ROW_SEMS + COL_SEMS + ACROSS,
        part_f, resid, part_b, dr, coming,
    )


def run_normed_back(part, resid, entry, gain):
    return call_remote(
        normed_back_kernel, 6, [TOKEN_WIDE, GAIN, ROW_BLOCKS],
        sum_col_scratch(D) + ROW_SEMS + COL_SEMS, part, resid, entry, gain,
    )


def run_input_back(part, dr, coming):
    return call_remote(
        input_back_kernel, 7, [TOKEN_ROWS, TOKEN_ROWS, COL_BLOCKS],
        ARRIVED + LAND_ROW + ROW_SEMS + COL_SEMS + ACROSS, part, dr, coming,
    )


def run_last(part_x, dr, part, gains):
    width = part.shape[-1]
    return call_remote(
        last_kernel, 8, [TOKEN_ROWS, sds((TOK, width), F32), sds((2, D), F32)],
        LAND_ROW + sum_col_scratch(width)
        + [pltpu.VMEM((2, D), F32), pltpu.VMEM((8, 2, D), F32), pltpu.VMEM((4, 2, D), F32)]
        + ROW_SEMS + COL_SEMS + [DMA((11,)), DMA((11,))],
        part_x, dr, part, gains,
    )


def swap_halves(value):
    width = value.shape[1]
    lane = lax.broadcasted_iota(jnp.int32, value.shape, 1)
    low = lax.rem(lane, HEAD) < HEAD // 2
    up = pltpu.roll(value, HEAD // 2, axis=1)
    down = pltpu.roll(value, width - HEAD // 2, axis=1)
    return low, up, down


def rope(value, cosine, sine):
    low, up, down = swap_halves(value)
    return value * cosine + jnp.where(low, -down, up) * sine


def rope_back(value, cosine, sine):
    low, up, down = swap_halves(value * sine)
    return value * cosine + jnp.where(low, down, -up)


def allowed_mask(seg, seg_t):
    shape = (PACK, PACK)
    query = lax.broadcasted_iota(jnp.int32, shape, 0)
    key = lax.broadcasted_iota(jnp.int32, shape, 1)
    return (seg[...] == seg_t[...]) & (key <= query)


def probabilities(q, k, allowed):
    scores = jnp.where(allowed, dot_cols(q, k) * SCORE_MUL, -1e30)
    weights = jnp.exp(scores - jnp.max(scores, axis=1, keepdims=True))
    return weights / jnp.sum(weights, axis=1, keepdims=True)


def attention_kernel(x_ref, w, gain, cosine, sine, seg, seg_t, part, n1, q_out, kv_out, o_out):
    x = x_ref[...].astype(F32)
    scale = lax.rsqrt(jnp.mean(x * x, axis=1, keepdims=True) + NORM_EPS)
    normed = (x * scale * gain[...]).astype(BF)
    n1[...] = normed
    cos, sin = cosine[...], sine[...]
    pre = dot(normed, w[:, 0:512])
    q = jnp.concatenate(
        [rope(pre[:, 0:128], cos, sin), rope(pre[:, 128:256], cos, sin)], axis=1
    ).astype(BF)
    k = rope(pre[:, 256:384], cos, sin).astype(BF)
    v = pre[:, 384:512].astype(BF)
    q_out[...] = q
    kv_out[:, 0:128] = k
    kv_out[:, 128:256] = v
    allowed = allowed_mask(seg, seg_t)
    heads = []
    for head in range(4):
        at = (head // 2) * HEAD
        prob = probabilities(q[:, head * HEAD:(head + 1) * HEAD], k[:, at:at + HEAD], allowed)
        heads.append(dot(prob.astype(BF), v[:, at:at + HEAD]))
    mixed = jnp.concatenate(heads, axis=1).astype(BF)
    o_out[...] = mixed
    part[...] = dot_cols(mixed, w[:, 512:768]).astype(BF)


def attention_back_kernel(
    da, x_ref, w, gain, cosine, sine, seg, seg_t, q_ref, kv_ref, part, dp_out, dgain
):
    cos, sin = cosine[...], sine[...]
    do = dot(da[...], w[:, 512:768]).astype(BF)
    q = q_ref[...]
    kv = kv_ref[...]
    allowed = allowed_mask(seg, seg_t)
    dqs, dks, dvs = [], [None, None], [None, None]
    for head in range(4):
        group = head // 2
        at = group * HEAD
        qh = q[:, head * HEAD:(head + 1) * HEAD]
        kh = kv[:, at:at + HEAD]
        vh = kv[:, 128 + at:128 + at + HEAD]
        doh = do[:, head * HEAD:(head + 1) * HEAD]
        prob = probabilities(qh, kh, allowed)
        dv = dot_rows(prob.astype(BF), doh)
        dprob = dot_cols(doh, vh)
        ds = (prob * (dprob - jnp.sum(prob * dprob, axis=1, keepdims=True))).astype(BF)
        dqs.append(dot(ds, kh) * SCORE_MUL)
        dk = dot_rows(ds, qh) * SCORE_MUL
        dks[group] = dk if dks[group] is None else dks[group] + dk
        dvs[group] = dv if dvs[group] is None else dvs[group] + dv
    dp = jnp.concatenate(
        [
            rope_back(jnp.concatenate(dqs[0:2], axis=1), cos, sin),
            rope_back(jnp.concatenate(dqs[2:4], axis=1), cos, sin),
            rope_back(jnp.concatenate(dks, axis=1), cos, sin),
            jnp.concatenate(dvs, axis=1),
        ],
        axis=1,
    ).astype(BF)
    dp_out[...] = dp
    dn1 = dot_cols(dp, w[:, 0:512])
    x = x_ref[...].astype(F32)
    scale = lax.rsqrt(jnp.mean(x * x, axis=1, keepdims=True) + NORM_EPS)
    dgain[...] = jnp.sum(dn1 * x * scale, axis=0, keepdims=True)
    weighted = dn1 * gain[...]
    inner = jnp.mean(weighted * x, axis=1, keepdims=True)
    part[...] = (scale * weighted - x * (scale * scale * scale) * inner).astype(BF)


def place_rows(table, rows, out):
    for quad in range(QUADS):
        value = dot(table[quad], rows[quad * 256:(quad + 1) * 256, :]).astype(BF)
        out[0, quad * 96:(quad + 1) * 96, :] = value[0:96]
        out[1, quad * 96:(quad + 1) * 96, :] = value[96:192]


def return_rows(table, value, out):
    for quad in range(QUADS):
        out[quad * 256:(quad + 1) * 256, :] = dot(table[quad], value[quad]).astype(BF)


def keep_rows(out, expert, value):
    for quad in range(QUADS):
        out[quad, expert * 96:(expert + 1) * 96, :] = value[quad * 96:(quad + 1) * 96]


def experts_kernel(rows, table, table_t, gslot, wg, wu, wd, part, xs, g_out, u_out, kept):
    place_rows(table, rows, xs)
    for expert in range(2):
        x = xs[expert]
        g = dot(x, wg[expert])
        u = dot(x, wu[expert])
        g_out[expert] = g
        u_out[expert] = u
        z = (g * jax.nn.sigmoid(g) * u).astype(BF)
        y = dot(z, wd[expert]).astype(BF).astype(F32)
        keep_rows(kept, expert, (y * gslot[expert]).astype(BF))
    return_rows(table_t, kept, part)


def experts_back_kernel(
    rows, table, table_t, gslot, g_ref, u_ref, wg, wu, wd, part, dy_out, dgu_out, z_out, kept
):
    place_rows(table, rows, dy_out)
    for expert in range(2):
        dy = ((RESID_MUL * gslot[expert]) * dy_out[expert].astype(F32)).astype(BF)
        dy_out[expert] = dy
        dz = dot_cols(dy, wd[expert])
        g, u = g_ref[expert], u_ref[expert]
        sig = jax.nn.sigmoid(g)
        silu = g * sig
        z_out[expert] = (silu * u).astype(BF)
        dg = (dz * u * sig * (1.0 + g * (1.0 - sig))).astype(BF)
        du = (dz * silu).astype(BF)
        dgu_out[expert, :, 0:FF] = dg
        dgu_out[expert, :, FF:2 * FF] = du
        keep_rows(kept, expert, (dot_cols(dg, wg[expert]) + dot_cols(du, wu[expert])).astype(BF))
    return_rows(table_t, kept, part)


def expert_weights_kernel(xa, xb, ga, gb, za, zb, ya, yb, gate_up, down, gate_up_buf, down_buf, sems):
    copies = []
    for j in range(ROWS):
        span = slice(j * 256, (j + 1) * 256)
        for expert in range(2):
            both = dot_rows(xa[expert, :, span], ga[expert]) + dot_rows(xb[expert, :, span], gb[expert])
            both = both.astype(BF)
            gate_up_buf[j, 0, expert] = both[:, 0:FF]
            gate_up_buf[j, 1, expert] = both[:, FF:2 * FF]
            down_buf[j, expert] = (
                dot_rows(za[expert], ya[expert, :, span]) + dot_rows(zb[expert], yb[expert, :, span])
            ).astype(BF)
        for index, (source, target) in enumerate(((gate_up_buf, gate_up), (down_buf, down))):
            copy = pltpu.make_async_copy(source.at[j], target.at[j], sems.at[2 * j + index])
            copy.start()
            copies.append(copy)
    for copy in copies:
        copy.wait()


def attention_weights_kernel(na, nb, pa, pb, da_a, da_b, oa, ob, out):
    out[:, 0:512] = (dot_rows(na[...], pa[...]) + dot_rows(nb[...], pb[...])).astype(BF)
    out[:, 512:768] = (dot_rows(da_a[...], oa[...]) + dot_rows(da_b[...], ob[...])).astype(BF)


def call_local(kernel, outs, flops, *args, scratch=(), limit=20):
    return pl.pallas_call(
        kernel,
        out_shape=outs,
        in_specs=[VM] * len(args),
        out_specs=[VM] * len(outs),
        scratch_shapes=list(scratch),
        compiler_params=pltpu.CompilerParams(vmem_limit_bytes=limit * 2**20),
        cost_estimate=pl.CostEstimate(flops=flops, bytes_accessed=6 * 10**6, transcendentals=0),
    )(*args)


def run_attention(packed, w, gain, tables):
    return call_local(
        attention_kernel,
        [sds((PACK, D), BF), sds((PACK, D), BF), sds((PACK, 256), BF), sds((PACK, 256), BF), sds((PACK, 256), BF)],
        10**9, packed, w, gain, *tables,
    )


def run_attention_back(da, packed, w, gain, tables, q, kv):
    return call_local(
        attention_back_kernel,
        [sds((PACK, D), BF), sds((PACK, 512), BF), sds((1, D), F32)],
        10**9, da, packed, w, gain, *tables, q, kv,
    )


KEPT = [pltpu.VMEM((QUADS, 2 * 96, D), BF)]


def run_experts(rows, routing, mats):
    ff = sds((2, SLOTS, FF), F32)
    return call_local(
        experts_kernel, [sds((D, D), BF), sds((2, SLOTS, D), BF), ff, ff],
        4 * 10**9, rows, *routing, *mats, scratch=KEPT, limit=30,
    )


def run_experts_back(rows, routing, g, u, mats):
    wide = sds((2, SLOTS, D), BF)
    return call_local(
        experts_back_kernel, [sds((D, D), BF), wide, wide, sds((2, SLOTS, FF), BF)],
        4 * 10**9, rows, *routing, g, u, *mats, scratch=KEPT, limit=30,
    )


def run_expert_weights(*pairs):
    args = [item for pair in pairs for item in pair]
    outs = [sds((ROWS, 2, 2, 256, FF), BF), sds((ROWS, 2, FF, 256), BF)]
    return pl.pallas_call(
        expert_weights_kernel,
        out_shape=outs,
        in_specs=[VM] * len(args),
        out_specs=[pl.BlockSpec(memory_space=pl.ANY)] * 2,
        scratch_shapes=[pltpu.VMEM(item.shape, BF) for item in outs] + [DMA((2 * ROWS,))],
        compiler_params=pltpu.CompilerParams(vmem_limit_bytes=30 * 2**20),
        cost_estimate=pl.CostEstimate(flops=5 * 10**9, bytes_accessed=20 * 10**6, transcendentals=0),
    )(*args)


def layout_tables(length_row):
    ends_at = jnp.cumsum(length_row)
    places = jnp.arange(PACK, dtype=jnp.int32)
    passed = places[:, None] >= ends_at[None, :]
    segment = jnp.sum(passed.astype(jnp.int32), axis=1)
    starts = jnp.sum(jnp.where(passed, length_row[None, :], 0), axis=1)
    offset = (places - starts).astype(F32)
    frequency = ROPE_THETA ** (-(jnp.arange(HEAD // 2, dtype=F32) * 2.0 / HEAD))
    angles = offset[:, None] * frequency[None, :]
    cosine = jnp.tile(jnp.cos(angles), (1, 4))
    sine = jnp.tile(jnp.sin(angles), (1, 4))
    return (cosine, sine, segment[:, None], segment[None, :])


def routing_tables(route_all, gate_all, col):
    mine = col * 2 + jnp.arange(2, dtype=jnp.int32)
    same = route_all[None] == mine[:, None, None, None]
    chosen = jnp.any(same, axis=3)
    gate = jnp.sum(jnp.where(same, gate_all[None], 0.0), axis=3)
    before = (jnp.arange(TOK)[:, None] < jnp.arange(TOK)[None, :]).astype(BF)
    rank = jnp.einsum("est,tu->esu", chosen.astype(BF), before, preferred_element_type=F32)
    slot = jnp.where(chosen, rank, -1.0)
    onehot = slot[:, :, None, :] == jnp.arange(CAP, dtype=F32)[None, None, :, None]
    gslot = jnp.sum(jnp.where(onehot, gate[:, :, None, :], 0.0), axis=3)
    blocks = jnp.swapaxes(onehot.reshape(2, QUADS, 4, CAP, 1, TOK), 0, 1)
    diagonal = jnp.eye(4, dtype=jnp.bool_).reshape(1, 1, 4, 1, 4, 1)
    table = (blocks & diagonal).astype(BF).reshape(QUADS, 2 * 4 * CAP, 4 * TOK)
    return (table, jnp.swapaxes(table, 1, 2), gslot.reshape(2, SLOTS, 1))


def per_device(
    ends_in, q_weight, key_projection, value_projection, out_weight, attn_gain, moe_gain,
    gate_weight, up_weight, down_weight, routes, gates, lengths,
):
    section = lax.axis_index("section")
    col = lax.axis_index("col")
    ends = ends_in[0, :, 0]
    own = jnp.concatenate([q_weight[0], key_projection[0], value_projection[0], out_weight[0]], axis=1)
    mine = jnp.concatenate([routes[0, :, 0].astype(F32).reshape(8, 128), gates[0, :, 0].reshape(8, 128)], axis=0)
    weights, shared, packed0 = run_start(own, mine, ends[0])
    weights = weights.reshape(D, 768)
    route_all = shared[:, 0:8].reshape(COLS, 2, TOK, 8).astype(jnp.int32)
    gate_all = shared[:, 8:16].reshape(COLS, 2, TOK, 8)
    mats = (gate_weight[0], up_weight[0], down_weight[0])
    attn_row, moe_row = attn_gain, moe_gain
    layouts, routings = [], []
    for micro in (section, 1 - section):
        layouts.append(layout_tables(lax.dynamic_index_in_dim(lengths[:, 0], micro, 0, keepdims=False)))
        routings.append(
            routing_tables(
                lax.dynamic_index_in_dim(route_all, micro, 1, keepdims=False),
                lax.dynamic_index_in_dim(gate_all, micro, 1, keepdims=False),
                col,
            )
        )

    kept = {}

    def forward_attention(step, packed):
        flat = packed.reshape(PACK, D)
        part, n1, q, kv, mixed = run_attention(flat, weights, attn_row, layouts[step % 2])
        kept[step] = [flat, n1, q, kv, mixed]
        return part.reshape(ROWS, TOK, D)

    def forward_experts(step, resid, rows):
        part, xs, g, u = run_experts(rows.reshape(D, D), routings[step % 2], mats)
        kept[step] += [resid, xs, g, u]
        return part.reshape(COLS, TOK, D)

    pieces, moe_gains, attn_gains = {}, {}, {}

    def backward_experts(step, grad_all):
        flat, n1, q, kv, mixed, resid, xs, g, u = kept[1 + step % 2]
        part, dy, dgu, z = run_experts_back(grad_all.reshape(D, D), routings[(step + 1) % 2], g, u, mats)
        pieces[step] = (xs, dgu, z, dy)
        return part.reshape(COLS, TOK, D), resid

    def backward_attention(step, da):
        flat, n1, q, kv, mixed = kept[1 + step % 2][0:5]
        da = da.reshape(PACK, D)
        part, dp, attn_gains[step] = run_attention_back(
            da, flat, weights, attn_row, layouts[(step + 1) % 2], q, kv
        )
        pieces[step] += (n1, dp, da, mixed)
        return part.reshape(ROWS, TOK, D)

    def both(items):
        return [item for pair in zip(*items) for item in pair]

    part = forward_attention(0, packed0)
    resid, grad_rows = run_first_attended(part, packed0, moe_row, ends[0])
    part = forward_experts(0, resid, grad_rows)
    _, packed = run_mixed(part, resid, ends[1])

    part = forward_attention(1, packed)
    resid, rows = run_attended(part, packed, moe_row)
    part = forward_experts(1, resid, rows)
    forward_one, packed = run_mixed(part, resid, ends[0])

    part = forward_attention(2, packed)
    part_b, resid_b = backward_experts(0, grad_rows)
    resid, rows, dr, _, da = run_turn_one(part, packed, part_b, resid_b, ends[0], moe_row)
    part = forward_experts(2, resid, rows)
    part_b = backward_attention(0, da)
    forward_two, _, entry, grad_rows = run_turn_two(part, resid, part_b, dr, ends[1])

    part, resid = backward_experts(1, grad_rows)
    dr, moe_gains[1], da = run_normed_back(part, resid, entry, moe_row)
    part = backward_attention(1, da)
    backward_one, entry, grad_rows = run_input_back(part, dr, ends[0])

    part, resid = backward_experts(2, grad_rows)
    gate_up, down = run_expert_weights(*zip(pieces[1][0:4], pieces[2][0:4]))
    gate_up = lax.psum_scatter(gate_up, "row", scatter_dimension=0, tiled=True)
    down = lax.psum_scatter(down, "row", scatter_dimension=0, tiled=True)
    dr, moe_gains[2], da = run_normed_back(part, resid, entry, moe_row)
    part_x = backward_attention(2, da)
    attn_part = call_local(
        attention_weights_kernel, [sds((D, 768), BF)], 10**9, *both((pieces[1][4:], pieces[2][4:]))
    )[0]
    gains = jnp.concatenate([attn_gains[1] + attn_gains[2], moe_gains[1] + moe_gains[2]], axis=0)
    backward_two, attn_sum, gain_sum = run_last(part_x, dr, attn_part.reshape(COLS, TOK, 768), gains)
    on_first = section == 0
    ends_out = jnp.stack(
        [jnp.where(on_first, backward_one, forward_one), jnp.where(on_first, backward_two, forward_two)], axis=0
    )[None, :, None]
    gate_up = gate_up.astype(F32)
    return (
        ends_out,
        attn_sum[None, :, 0:256],
        attn_sum[None, :, 256:384],
        attn_sum[None, :, 384:512],
        attn_sum[None, :, 512:768],
        gain_sum[0:1],
        gain_sum[1:2],
        gate_up[:, 0],
        gate_up[:, 1],
        down.astype(F32),
    )


def solution(mesh):
    tokens = P("section", None, "col", "row", None)
    mats = P("section", "col", "row")
    gain = P("section", None)
    experts = P("section", "col", None, None)
    by_row = P("section", "col", "row", None)
    return jax.shard_map(
        per_device,
        mesh=mesh,
        in_specs=(tokens, mats, mats, mats, mats, gain, gain, experts, experts, experts, tokens, tokens, P(None, "col", None)),
        out_specs=(tokens, mats, mats, mats, mats, gain, gain, by_row, by_row, P("section", "col", None, "row")),
        check_vma=False,
    )
```

time: 565 us -> 457 us (0.81)
  Pallas kernels: 498 us -> 368 us
  waiting for transfers between devices: 0.02 us -> 21.2 us
    pallas_call x14 -> x11, Pallas kernels: 396 us -> 317 us  [call_remote(): pl.pallas_call(kernel, out_shape=outs, in_specs=[VM] * len(args), out_spe...]
    pallas_call x7 -> x1, Pallas kernels: 84.8 us -> 8.07 us  [run_expert_weights(): pl.pallas_call(expert_weights_kernel, out_shape=outs, in_specs=[VM] * len...]
    pallas_call x7 -> x13, Pallas kernels: 17.6 us -> 42.5 us  [call_local(): pl.pallas_call(kernel, out_shape=outs, in_specs=[VM] * len(args), out_spe...]
    reduce_scatter x1 -> x2, waiting for transfers between devices: 0.01 us -> 20.5 us  [the longest x1 20.5 us: per_device(): gate_up = lax.psum_scatter(gate_up, 'row', scatter_dimension=0, tiled=True)]
    unnamed x130 -> x139, local copies, waits for them, and re-layouts: 28.6 us -> 14.7 us
  transfers between devices with their start and end apart: 1 -> 2, of which waited for: 0 -> 1; matrix products, arithmetic and copies ran while one was open for 0% -> 1% of each run, Pallas kernels for 14% -> 12%
where the time goes in v2:
time: 457 us; the launch traced here: 448 us
  Pallas kernels  368 us (81%)
  local copies, waits for them, and re-layouts  33.8 us (7%)
  waiting for transfers between devices  21.2 us (5%)
  between operations  15.8 us (3%)
  other arithmetic  8.7 us (2%)
    pallas_call x11, Pallas kernels, call_remote(): pl.pallas_call(kernel, out_shape=outs, in_specs=[VM] * len(args), out_spe...  317 us
    pallas_call x13, Pallas kernels, call_local(): pl.pallas_call(kernel, out_shape=outs, in_specs=[VM] * len(args), out_spe...  42.5 us
    reduce_scatter x1, waiting for transfers between devices, per_device(): gate_up = lax.psum_scatter(gate_up, 'row', scatter_dimension=0, tiled=True)  20.5 us
    unnamed x139, local copies, waits for them, and re-layouts  14.7 us
  transfers between devices with their start and end apart: 2, of which 1 were waited for; matrix products, arithmetic and copies ran while one was open for 1% of the time, Pallas kernels for 12%

profile of v2, /device:TPU:1, one launch (start us, length us, event | category | flops | bytes accessed | tf_op | source)
XLA Modules:
  0.0 447.6 jit_solution(7733863018875748772)
XLA Ops:
  7.3 0.7 fusion.9
  8.5 0.7 convert_element_type.51
  9.4 0.8 copy.167
  10.4 0.8 and.50
  11.8 0.8 copy.181.seg
  12.6 0.7 copy.179.cosine
  13.7 20.7 %shard_map.204 = (bf16[16,64,768]{2,1,0:T(8,128)(2,1)S(1)}, f32[16,16,128]{2,1,0:T(8,128)S(1)}, bf16[4,64,1024]{2,1,0:T(8,128)(2,1)S(1)}) custom-call(bf16[64,768]{1,0:T(8,128)(2,1)S(1)} %pad_maximum_fusion.w_ref, f32[16,128]{1,0:T(8,128)S(1)} %pad_maximum_fusion.1.rg_ref, bf16[64,1024]{1,0:T(8,128)(2,1)S(1)} %get-tuple-element.211.x_ref.other.coming.entry), custom_call_target="tpu_custom_call" | custom-call | flops 1000000 | bytes 40000000 | tf_op jit(solution)/shard_map/pallas_call | solution.py:398
  34.4 1.3 copy.175
  35.7 1.1 constant_dynamic-slice_fusion.2
  36.8 0.8 copy.176
  37.6 0.8 copy.185
  38.3 1.0 copy.171
  39.4 1.1 constant_dynamic-slice_fusion.3
  41.8 0.6 and.55
  43.3 1.0 broadcast_and_fusion
  45.9 0.9 reshape.390.gslot
  47.1 0.9 convert_bitcast_fusion
  48.1 1.4 copy.186.table
  49.6 1.5 copy-done.50
  51.1 2.7 shard_map.205
  53.7 25.7 %shard_map.206 = (f32[64,1024]{1,0:T(8,128)S(1)}, bf16[16,64,1024]{2,1,0:T(8,128)(2,1)S(1)}) custom-call(bf16[4,64,1024]{2,1,0:T(8,128)(2,1)S(1)} %bitcast.125, bf16[4,64,1024]{2,1,0:T(8,128)(2,1)S(1)} %get-tuple-element.77.packed, f32[1,1024]{1,0:T(1,128)S(1)} %copy-done.42, bf16[64,1024]{1,0:T(8,128)(2,1)S(1)} %get-tuple-element.211.x_ref.other.coming.entry), custom_call_target="tpu_custom_call" | custom-call | flops 1000000 | bytes 40000000 | tf_op jit(solution)/shard_map/pallas_call | solution.py:398
  79.5 1.6 copy-done.47
  81.1 4.5 %shard_map.207 = (bf16[1024,1024]{1,0:T(8,128)(2,1)S(1)}, bf16[2,384,1024]{2,1,0:T(8,128)(2,1)}, f32[2,384,512]{2,1,0:T(8,128)}, f32[2,384,512]{2,1,0:T(8,128)}) custom-call(bf16[1024,1024]{1,0:T(8,128)(2,1)S(1)} %bitcast.157, bf16[4,192,256]{2,1,0:T(8,128)(2,1)S(1)} %copy.177.table, bf16[4,256,192]{2,1,0:T(8,128)(2,1)S(1)} %get-tuple-element.212.table_t, ...), custom_call_target="tpu_custom_call" | custom-call | flops 4000000000 | bytes 6000000 | tf_op jit(solution)/shard_map/pallas_call | solution.py:671
  85.6 29.2 %shard_map.208 = (bf16[64,1024]{1,0:T(8,128)(2,1)}, bf16[4,64,1024]{2,1,0:T(8,128)(2,1)S(1)}) custom-call(bf16[16,64,1024]{2,1,0:T(8,128)(2,1)S(1)} %bitcast.111, f32[64,1024]{1,0:T(8,128)S(1)} %get-tuple-element.83.resid, bf16[64,1024]{1,0:T(8,128)(2,1)S(1)} %get-tuple-element.210.coming), custom_call_target="tpu_custom_call" | custom-call | flops 1000000 | bytes 40000000 | tf_op jit(solution)/shard_map/pallas_call | solution.py:398
  114.8 2.0 shard_map.209
  116.9 26.7 %shard_map.210 = (f32[64,1024]{1,0:T(8,128)S(1)}, bf16[16,64,1024]{2,1,0:T(8,128)(2,1)S(1)}) custom-call(bf16[4,64,1024]{2,1,0:T(8,128)(2,1)S(1)} %bitcast.126, bf16[4,64,1024]{2,1,0:T(8,128)(2,1)S(1)} %get-tuple-element.84.packed, f32[1,1024]{1,0:T(1,128)S(1)} %copy-done.42), custom_call_target="tpu_custom_call" | custom-call | flops 1000000 | bytes 40000000 | tf_op jit(solution)/shard_map/pallas_call | solution.py:398
  143.7 3.7 shard_map.211
  147.4 1.2 copy-done.60
  148.6 27.6 %shard_map.212 = (bf16[64,1024]{1,0:T(8,128)(2,1)S(1)}, bf16[4,64,1024]{2,1,0:T(8,128)(2,1)S(1)}) custom-call(bf16[16,64,1024]{2,1,0:T(8,128)(2,1)S(1)} %bitcast.112, f32[64,1024]{1,0:T(8,128)S(1)} %get-tuple-element.88.resid.resid_b, bf16[64,1024]{1,0:T(8,128)(2,1)S(1)} %get-tuple-element.211.x_ref.other.coming.entry), custom_call_target="tpu_custom_call" | custom-call | flops 1000000 | bytes 40000000 | tf_op jit(solution)/shard_map/pallas_call | solution.py:398
  176.2 0.6 copy-done.36
  176.9 2.0 shard_map.213
  178.9 0.6 copy-done.19
  179.5 4.8 %shard_map.214 = (bf16[1024,1024]{1,0:T(8,128)(2,1)S(1)}, bf16[2,384,1024]{2,1,0:T(8,128)(2,1)}, bf16[2,384,1024]{2,1,0:T(8,128)(2,1)}, bf16[2,384,512]{2,1,0:T(8,128)(2,1)}) custom-call(bf16[1024,1024]{1,0:T(8,128)(2,1)S(1)} %bitcast.158, bf16[4,192,256]{2,1,0:T(8,128)(2,1)S(1)} %copy.186.table, bf16[4,256,192]{2,1,0:T(8,128)(2,1)S(1)} %get-tuple-element.208.table_t, ...), custom_call_target="tpu_custom_call" | custom-call | flops 4000000000 | bytes 6000000 | tf_op jit(solution)/shard_map/pallas_call | solution.py:671
  184.3 44.8 %shard_map.215 = (f32[64,1024]{1,0:T(8,128)S(1)}, bf16[16,64,1024]{2,1,0:T(8,128)(2,1)S(1)}, f32[64,1024]{1,0:T(8,128)S(1)}, f32[1,1024]{1,0:T(1,128)}, bf16[4,64,1024]{2,1,0:T(8,128)(2,1)S(1)}) custom-call(bf16[4,64,1024]{2,1,0:T(8,128)(2,1)S(1)} %bitcast.130, bf16[4,64,1024]{2,1,0:T(8,128)(2,1)S(1)} %get-tuple-element.89.packed, ...), custom_call_target="tpu_custom_call" | custom-call | flops 1000000 | bytes 40000000 | tf_op jit(solution)/shard_map/pallas_call | solution.py:398
  229.1 3.7 shard_map.216
  232.9 3.6 shard_map.217
  236.5 36.3 %shard_map.218 = (bf16[64,1024]{1,0:T(8,128)(2,1)S(1)}, bf16[64,1024]{1,0:T(8,128)(2,1)}, bf16[64,1024]{1,0:T(8,128)(2,1)S(1)}, bf16[16,64,1024]{2,1,0:T(8,128)(2,1)S(1)}) custom-call(bf16[16,64,1024]{2,1,0:T(8,128)(2,1)S(1)} %bitcast.113, f32[64,1024]{1,0:T(8,128)S(1)} %get-tuple-element.96.resid, bf16[4,64,1024]{2,1,0:T(8,128)(2,1)S(1)} %bitcast.119, ...), custom_call_target="tpu_custom_call" | custom-call | flops 1000000 | bytes 40000000 | tf_op jit(solution)/shard_map/pallas_call | solution.py:398
  272.8 4.2 shard_map.219
  277.0 25.3 %shard_map.220 = (f32[64,1024]{1,0:T(8,128)S(1)}, f32[1,1024]{1,0:T(1,128)S(1)}, bf16[4,64,1024]{2,1,0:T(8,128)(2,1)S(1)}) custom-call(bf16[16,64,1024]{2,1,0:T(8,128)(2,1)S(1)} %bitcast.110, f32[64,1024]{1,0:T(8,128)S(1)} %get-tuple-element.96.resid, bf16[64,1024]{1,0:T(8,128)(2,1)S(1)} %get-tuple-element.106.entry, f32[1,1024]{1,0:T(1,128)S(1)} %copy-done.42), custom_call_target="tpu_custom_call" | custom-call | flops 1000000 | bytes 40000000 | tf_op jit(solution)/shard_map/pallas_call | solution.py:398
  302.4 3.0 shard_map.221
  305.4 0.8 copy-done.2
  306.2 0.7 copy-done.15
  306.9 29.3 %shard_map.222 = (bf16[64,1024]{1,0:T(8,128)(2,1)S(1)}, bf16[64,1024]{1,0:T(8,128)(2,1)S(1)}, bf16[16,64,1024]{2,1,0:T(8,128)(2,1)S(1)}) custom-call(bf16[4,64,1024]{2,1,0:T(8,128)(2,1)S(1)} %bitcast.120, f32[64,1024]{1,0:T(8,128)S(1)} %get-tuple-element.111.dr, bf16[64,1024]{1,0:T(8,128)(2,1)S(1)} %get-tuple-element.211.x_ref.other.coming.entry), custom_call_target="tpu_custom_call" | custom-call | flops 1000000 | bytes 40000000 | tf_op jit(solution)/shard_map/pallas_call | solution.py:398
  336.2 0.6 copy-done.21
  336.9 0.7 copy-done.40
  337.6 4.2 shard_map.223
  341.7 8.1 %shard_map.228 = (bf16[4,2,2,256,512]{4,3,2,1,0:T(8,128)(2,1)S(1)}, bf16[4,2,512,256]{3,2,1,0:T(8,128)(2,1)S(1)}) custom-call(bf16[2,384,1024]{2,1,0:T(8,128)(2,1)S(1)} %get-tuple-element.134.xa, bf16[2,384,1024]{2,1,0:T(8,128)(2,1)S(1)} %copy-done.61, bf16[2,384,1024]{2,1,0:T(8,128)(2,1)S(1)} %get-tuple-element.136.ga, ...), custom_call_target="tpu_custom_call" | custom-call | flops 5000000000 | bytes 20000000 | tf_op jit(solution)/shard_map/pallas_call | solution.py:720
  349.8 2.0 copy-done
  351.8 1.3 copy-done.1
  353.2 0.7 reduce-scatter.3.cloned.1.call-update
  354.1 29.9 %shard_map.224 = (f32[64,1024]{1,0:T(8,128)S(1)}, f32[1,1024]{1,0:T(1,128)S(1)}, bf16[4,64,1024]{2,1,0:T(8,128)(2,1)S(1)}) custom-call(bf16[16,64,1024]{2,1,0:T(8,128)(2,1)S(1)} %bitcast.109, f32[64,1024]{1,0:T(8,128)S(1)} %get-tuple-element.88.resid.resid_b, bf16[64,1024]{1,0:T(8,128)(2,1)S(1)} %copy-done.22, f32[1,1024]{1,0:T(1,128)S(1)} %copy-done.42), custom_call_target="tpu_custom_call" | custom-call | flops 1000000 | bytes 40000000 | tf_op jit(solution)/shard_map/pallas_call | solution.py:398
  384.2 1.0 copy-done.57
  385.1 0.9 copy-done.59
  386.1 3.0 shard_map.225
  389.2 1.1 shard_map.226
  390.3 21.8 %shard_map.227 = (bf16[64,1024]{1,0:T(8,128)(2,1)S(1)}, f32[64,768]{1,0:T(8,128)S(1)}, f32[2,1024]{1,0:T(2,128)S(1)}) custom-call(bf16[4,64,1024]{2,1,0:T(8,128)(2,1)S(1)} %bitcast.129, f32[64,1024]{1,0:T(8,128)S(1)} %get-tuple-element.119.dr, bf16[16,64,768]{2,1,0:T(8,128)(2,1)S(1)} %bitcast.108, f32[2,1024]{1,0:T(2,128)S(1)} %pad_maximum_fusion.2.gains), custom_call_target="tpu_custom_call" | custom-call | flops 1000000 | bytes 40000000 | tf_op jit(solution)/shard_map/pallas_call | solution.py:398
  412.2 0.7 maximum_bitcast_fusion
  412.9 0.6 fusion.12
  413.5 0.6 slice_bitcast_fusion.6
  414.1 0.7 slice_bitcast_fusion.4
  414.8 2.1 convert_element_type.62
  416.9 20.5 %reduce-scatter.3.cloned.1.call-done = bf16[1,2,2,256,512]{4,3,2,1,0:T(8,128)(2,1)} async-done(((bf16[4,2,2,256,512]{4,3,2,1,0:T(8,128)(2,1)}), bf16[1,2,2,256,512]{4,3,2,1,0:T(8,128)(2,1)}) %reduce-scatter.3.cloned.1.call-update) | async-done | bytes 1048592 | tf_op jit(solution)/shard_map/reduce_scatter | solution.py:844
  437.4 1.5 convert_element_type.61
  438.9 1.5 slice_bitcast_fusion
  (176 shorter events, 6.3 us)
Async XLA Ops:
  7.2 6.4 %copy-start.62 = (bf16[1,2,1,64,1024]{4,3,2,1,0:T(8,128)(2,1)S(1)}, bf16[1,2,1,64,1024]{4,3,2,1,0:T(8,128)(2,1)}, u32[]{:S(2)}) copy-start(bf16[1,2,1,64,1024]{4,3,2,1,0:T(8,128)(2,1)} %param.13) | copy-start | bytes 786436
  7.2 6.5 %copy-start.65 = (bf16[1,64,256]{2,1,0:T(8,128)(2,1)S(1)}, bf16[1,64,256]{2,1,0:T(8,128)(2,1)}, u32[]{:S(2)}) copy-start(bf16[1,64,256]{2,1,0:T(8,128)(2,1)} %param.17) | copy-start | bytes 98308
  7.2 6.5 %copy-start.67 = (bf16[1,64,128]{2,1,0:T(8,128)(2,1)S(1)}, bf16[1,64,128]{2,1,0:T(8,128)(2,1)}, u32[]{:S(2)}) copy-start(bf16[1,64,128]{2,1,0:T(8,128)(2,1)} %param.16) | copy-start | bytes 49156
  7.2 6.5 %copy-start.68 = (bf16[1,64,128]{2,1,0:T(8,128)(2,1)S(1)}, bf16[1,64,128]{2,1,0:T(8,128)(2,1)}, u32[]{:S(2)}) copy-start(bf16[1,64,128]{2,1,0:T(8,128)(2,1)} %param.15) | copy-start | bytes 49156
  7.2 6.5 %copy-start.66 = (bf16[1,64,256]{2,1,0:T(8,128)(2,1)S(1)}, bf16[1,64,256]{2,1,0:T(8,128)(2,1)}, u32[]{:S(2)}) copy-start(bf16[1,64,256]{2,1,0:T(8,128)(2,1)} %param.14) | copy-start | bytes 98308
  7.2 407.6 %reduce-scatter.5.cloned.1.call-start = ((), (), s32[]{:S(2)}) async-start(), calls=%async_computation.3 | async-start | bytes 2621440 | tf_op jit(solution)/shard_map/reduce_scatter | solution.py:845
  11.6 103.2 %copy-start.23 = (f32[256,128]{1,0:T(8,128)}, f32[256,128]{1,0:T(8,128)S(1)}, u32[]{:S(2)}) copy-start(f32[256,128]{1,0:T(8,128)S(1)} %copy.180.sine) | copy-start | bytes 393220
  11.8 37.7 %copy-start.30 = (s32[256,1]{1,0:T(8,128)}, s32[256,1]{1,0:T(8,128)S(1)}, u32[]{:S(2)}) copy-start(s32[256,1]{1,0:T(8,128)S(1)} %copy.170.seg) | copy-start | bytes 3076
  13.5 36.0 %copy-start.32 = (f32[256,128]{1,0:T(8,128)}, f32[256,128]{1,0:T(8,128)S(1)}, u32[]{:S(2)}) copy-start(f32[256,128]{1,0:T(8,128)S(1)} %copy.168.cosine) | copy-start | bytes 393220
  13.6 35.9 %copy-start.34 = (f32[256,128]{1,0:T(8,128)}, f32[256,128]{1,0:T(8,128)S(1)}, u32[]{:S(2)}) copy-start(f32[256,128]{1,0:T(8,128)S(1)} %copy.169.sine) | copy-start | bytes 393220
  34.4 6.0 %copy-start.49 = (bf16[16,64,768]{2,1,0:T(8,128)(2,1)}, bf16[16,64,768]{2,1,0:T(8,128)(2,1)S(1)}, u32[]{:S(2)}) copy-start(bf16[16,64,768]{2,1,0:T(8,128)(2,1)S(1)} %get-tuple-element.78) | copy-start | bytes 4718596
  40.9 4.3 copy-start.63
  40.9 4.3 copy-start.64
  45.9 97.8 %copy-start.12 = (f32[2,384,1]{2,1,0:T(8,128)}, f32[2,384,1]{2,1,0:T(8,128)S(1)}, u32[]{:S(2)}) copy-start(f32[2,384,1]{2,1,0:T(8,128)S(1)} %reshape.391.gslot) | copy-start | bytes 9220
  46.8 2.7 copy-start.53
  47.1 32.3 %copy-start.10 = (bf16[4,192,256]{2,1,0:T(8,128)(2,1)}, bf16[4,192,256]{2,1,0:T(8,128)(2,1)S(1)}, u32[]{:S(2)}) copy-start(bf16[4,192,256]{2,1,0:T(8,128)(2,1)S(1)} %copy.177.table) | copy-start | bytes 1179652
  48.0 131.5 %copy-start.6 = (bf16[4,256,192]{2,1,0:T(8,128)(2,1)}, bf16[4,256,192]{2,1,0:T(8,128)(2,1)S(1)}, u32[]{:S(2)}) copy-start(bf16[4,256,192]{2,1,0:T(8,128)(2,1)S(1)} %get-tuple-element.208.table_t) | copy-start | bytes 1179652
  48.0 5.7 %copy-start.42 = (f32[1,1024]{1,0:T(1,128)S(1)}, f32[1,1024]{1,0:T(1,128)}, u32[]{:S(2)}) copy-start(f32[1,1024]{1,0:T(1,128)} %gain.20) | copy-start | bytes 12292
  49.5 130.0 %copy-start.8 = (bf16[4,192,256]{2,1,0:T(8,128)(2,1)}, bf16[4,192,256]{2,1,0:T(8,128)(2,1)S(1)}, u32[]{:S(2)}) copy-start(bf16[4,192,256]{2,1,0:T(8,128)(2,1)S(1)} %copy.186.table) | copy-start | bytes 1179652
  49.6 1.5 copy-start.50
  51.1 28.4 %copy-start.14 = (f32[2,384,1]{2,1,0:T(8,128)S(1)}, f32[2,384,1]{2,1,0:T(8,128)}, u32[]{:S(2)}) copy-start(f32[2,384,1]{2,1,0:T(8,128)} %reshape.390.gslot) | copy-start | bytes 9220
  51.1 28.4 %copy-start.45 = (bf16[1,2,1024,512]{3,2,1,0:T(8,128)(2,1)S(1)}, bf16[1,2,1024,512]{3,2,1,0:T(8,128)(2,1)}, u32[]{:S(2)}) copy-start(bf16[1,2,1024,512]{3,2,1,0:T(8,128)(2,1)} %param.20) | copy-start | bytes 6291460
  51.1 28.4 %copy-start.46 = (bf16[1,2,1024,512]{3,2,1,0:T(8,128)(2,1)S(1)}, bf16[1,2,1024,512]{3,2,1,0:T(8,128)(2,1)}, u32[]{:S(2)}) copy-start(bf16[1,2,1024,512]{3,2,1,0:T(8,128)(2,1)} %param.21) | copy-start | bytes 6291460
  79.5 1.6 copy-start.47
  85.6 29.2 %copy-start.26 = (s32[256,1]{1,0:T(8,128)S(1)}, s32[256,1]{1,0:T(8,128)}, u32[]{:S(2)}) copy-start(s32[256,1]{1,0:T(8,128)} %copy.181.seg) | copy-start | bytes 3076
  85.6 29.2 %copy-start.28 = (f32[256,128]{1,0:T(8,128)S(1)}, f32[256,128]{1,0:T(8,128)}, u32[]{:S(2)}) copy-start(f32[256,128]{1,0:T(8,128)} %copy.179.cosine) | copy-start | bytes 393220
  85.6 29.2 %copy-start.51 = (bf16[16,64,768]{2,1,0:T(8,128)(2,1)S(1)}, bf16[16,64,768]{2,1,0:T(8,128)(2,1)}, u32[]{:S(2)}) copy-start(bf16[16,64,768]{2,1,0:T(8,128)(2,1)} %copy-done.49) | copy-start | bytes 4718596
  114.8 118.1 %copy-start.4 = (bf16[4,64,1024]{2,1,0:T(8,128)(2,1)}, bf16[4,64,1024]{2,1,0:T(8,128)(2,1)S(1)}, u32[]{:S(2)}) copy-start(bf16[4,64,1024]{2,1,0:T(8,128)(2,1)S(1)} %get-tuple-element.84.packed) | copy-start | bytes 1572868
  116.9 26.8 %copy-start.17 = (bf16[256,256]{1,0:T(8,128)(2,1)}, bf16[256,256]{1,0:T(8,128)(2,1)S(1)}, u32[]{:S(2)}) copy-start(bf16[256,256]{1,0:T(8,128)(2,1)S(1)} %get-tuple-element.125.ob) | copy-start | bytes 393220
  116.9 116.0 %copy-start.56 = (bf16[256,256]{1,0:T(8,128)(2,1)}, bf16[256,256]{1,0:T(8,128)(2,1)S(1)}, u32[]{:S(2)}) copy-start(bf16[256,256]{1,0:T(8,128)(2,1)S(1)} %get-tuple-element.98.q_ref) | copy-start | bytes 393220
  116.9 116.0 %copy-start.58 = (bf16[256,256]{1,0:T(8,128)(2,1)}, bf16[256,256]{1,0:T(8,128)(2,1)S(1)}, u32[]{:S(2)}) copy-start(bf16[256,256]{1,0:T(8,128)(2,1)S(1)} %get-tuple-element.99.kv_ref) | copy-start | bytes 393220
  147.4 1.2 copy-start.60
  148.6 28.3 %copy-start.31 = (s32[256,1]{1,0:T(8,128)S(1)}, s32[256,1]{1,0:T(8,128)}, u32[]{:S(2)}) copy-start(s32[256,1]{1,0:T(8,128)} %copy-done.30) | copy-start | bytes 3076
  148.6 28.3 %copy-start.33 = (f32[256,128]{1,0:T(8,128)S(1)}, f32[256,128]{1,0:T(8,128)}, u32[]{:S(2)}) copy-start(f32[256,128]{1,0:T(8,128)} %copy-done.32) | copy-start | bytes 393220
  148.6 28.3 %copy-start.35 = (f32[256,128]{1,0:T(8,128)S(1)}, f32[256,128]{1,0:T(8,128)}, u32[]{:S(2)}) copy-start(f32[256,128]{1,0:T(8,128)} %copy-done.34) | copy-start | bytes 393220
  176.8 2.7 copy-start.13
  176.8 2.7 copy-start.48
  184.3 44.8 %copy-start.11 = (bf16[4,192,256]{2,1,0:T(8,128)(2,1)S(1)}, bf16[4,192,256]{2,1,0:T(8,128)(2,1)}, u32[]{:S(2)}) copy-start(bf16[4,192,256]{2,1,0:T(8,128)(2,1)} %copy-done.10) | copy-start | bytes 1179652
  229.1 3.8 copy-start.24
  272.8 4.2 copy-start.38
  277.0 25.3 %copy-start.54 = (f32[1,1024]{1,0:T(1,128)S(1)}, f32[1,1024]{1,0:T(1,128)}, u32[]{:S(2)}) copy-start(f32[1,1024]{1,0:T(1,128)} %gain.21) | copy-start | bytes 12292
  302.3 33.9 %copy-start.43 = (f32[1,1024]{1,0:T(1,128)}, f32[1,1024]{1,0:T(1,128)S(1)}, u32[]{:S(2)}) copy-start(f32[1,1024]{1,0:T(1,128)S(1)} %get-tuple-element.128) | copy-start | bytes 12292
  302.3 35.2 %copy-start.7 = (bf16[4,256,192]{2,1,0:T(8,128)(2,1)S(1)}, bf16[4,256,192]{2,1,0:T(8,128)(2,1)}, u32[]{:S(2)}) copy-start(bf16[4,256,192]{2,1,0:T(8,128)(2,1)} %copy-done.6) | copy-start | bytes 1179652
  302.4 35.2 %copy-start.9 = (bf16[4,192,256]{2,1,0:T(8,128)(2,1)S(1)}, bf16[4,192,256]{2,1,0:T(8,128)(2,1)}, u32[]{:S(2)}) copy-start(bf16[4,192,256]{2,1,0:T(8,128)(2,1)} %copy-done.8) | copy-start | bytes 1179652
  337.6 4.2 copy-start.61
  349.8 2.0 copy-start
  351.8 1.3 copy-start.1
  353.1 84.2 %reduce-scatter.3.cloned.1.call-start = ((), (), s32[]{:S(2)}) async-start(), calls=%async_computation.2 | async-start | bytes 5242880 | tf_op jit(solution)/shard_map/reduce_scatter | solution.py:844
  353.9 30.2 %copy-start.44 = (f32[1,1024]{1,0:T(1,128)S(1)}, f32[1,1024]{1,0:T(1,128)}, u32[]{:S(2)}) copy-start(f32[1,1024]{1,0:T(1,128)} %copy-done.43) | copy-start | bytes 12292
  353.9 30.2 %copy-start.5 = (bf16[4,64,1024]{2,1,0:T(8,128)(2,1)S(1)}, bf16[4,64,1024]{2,1,0:T(8,128)(2,1)}, u32[]{:S(2)}) copy-start(bf16[4,64,1024]{2,1,0:T(8,128)(2,1)} %copy-done.4) | copy-start | bytes 1572868
  353.9 30.2 %copy-start.25 = (f32[256,128]{1,0:T(8,128)S(1)}, f32[256,128]{1,0:T(8,128)}, u32[]{:S(2)}) copy-start(f32[256,128]{1,0:T(8,128)} %copy-done.23) | copy-start | bytes 393220
  353.9 30.2 %copy-start.27 = (s32[256,1]{1,0:T(8,128)S(1)}, s32[256,1]{1,0:T(8,128)}, u32[]{:S(2)}) copy-start(s32[256,1]{1,0:T(8,128)} %copy.181.seg) | copy-start | bytes 3076
  353.9 30.2 %copy-start.29 = (f32[256,128]{1,0:T(8,128)S(1)}, f32[256,128]{1,0:T(8,128)}, u32[]{:S(2)}) copy-start(f32[256,128]{1,0:T(8,128)} %copy.179.cosine) | copy-start | bytes 393220
  354.0 30.2 %copy-start.52 = (bf16[16,64,768]{2,1,0:T(8,128)(2,1)S(1)}, bf16[16,64,768]{2,1,0:T(8,128)(2,1)}, u32[]{:S(2)}) copy-start(bf16[16,64,768]{2,1,0:T(8,128)(2,1)} %copy-done.49) | copy-start | bytes 4718596
  354.0 30.2 %copy-start.55 = (f32[1,1024]{1,0:T(1,128)S(1)}, f32[1,1024]{1,0:T(1,128)}, u32[]{:S(2)}) copy-start(f32[1,1024]{1,0:T(1,128)} %gain.21) | copy-start | bytes 12292
  384.0 5.1 %copy-start.3 = (bf16[4,64,1024]{2,1,0:T(8,128)(2,1)S(1)}, bf16[4,64,1024]{2,1,0:T(8,128)(2,1)}, u32[]{:S(2)}) copy-start(bf16[4,64,1024]{2,1,0:T(8,128)(2,1)} %copy-done.2) | copy-start | bytes 1572868
  384.0 5.1 %copy-start.16 = (bf16[256,512]{1,0:T(8,128)(2,1)S(1)}, bf16[256,512]{1,0:T(8,128)(2,1)}, u32[]{:S(2)}) copy-start(bf16[256,512]{1,0:T(8,128)(2,1)} %copy-done.15) | copy-start | bytes 786436
  384.1 5.1 %copy-start.18 = (bf16[256,256]{1,0:T(8,128)(2,1)S(1)}, bf16[256,256]{1,0:T(8,128)(2,1)}, u32[]{:S(2)}) copy-start(bf16[256,256]{1,0:T(8,128)(2,1)} %copy-done.17) | copy-start | bytes 393220
  384.1 5.1 %copy-start.20 = (bf16[256,256]{1,0:T(8,128)(2,1)S(1)}, bf16[256,256]{1,0:T(8,128)(2,1)}, u32[]{:S(2)}) copy-start(bf16[256,256]{1,0:T(8,128)(2,1)} %copy-done.19) | copy-start | bytes 393220
  384.2 1.0 copy-start.57
  385.1 0.9 copy-start.59
  390.2 21.8 %copy-start.37 = (bf16[64,1024]{1,0:T(8,128)(2,1)S(1)}, bf16[64,1024]{1,0:T(8,128)(2,1)}, u32[]{:S(2)}) copy-start(bf16[64,1024]{1,0:T(8,128)(2,1)} %copy-done.36) | copy-start | bytes 393220
  390.3 21.8 %copy-start.41 = (bf16[64,1024]{1,0:T(8,128)(2,1)S(1)}, bf16[64,1024]{1,0:T(8,128)(2,1)}, u32[]{:S(2)}) copy-start(bf16[64,1024]{1,0:T(8,128)(2,1)} %copy-done.40) | copy-start | bytes 393220
  390.3 21.9 %copy-start.39 = (bf16[64,1024]{1,0:T(8,128)(2,1)S(1)}, bf16[64,1024]{1,0:T(8,128)(2,1)}, u32[]{:S(2)}) copy-start(bf16[64,1024]{1,0:T(8,128)(2,1)} %copy-done.38) | copy-start | bytes 393220
  (7 other events, 5.0 us)
Sparse Core Ops, SparseCore 0:
  353.3 32.6 reduce-scatter.4
  388.5 48.7 reduce-scatter.2
